TPU v7x, 32 devices: a whole 2x2x4 slice. The times are simulated.
32 devices in a mesh: grp: 8 (over z, x), sp: 4 (over y, core).
Axes of the slice: x: 2, y: 2, z: 4, core: 2. Of those that a mesh axis runs over, the one named last changes fastest.
Arguments:
- queries: bfloat16 [5120, 4096], P(('grp', 'sp')), may hold values from -128 to 128
- fresh_key_values: bfloat16 [5120, 1024], P(('grp', 'sp')), may hold values from -4 to 4
- cache: bfloat16 [8, 4, 512, 256], P('grp', 'sp'), may hold values from -4 to 4
- lengths: int32 [8, 4], P('grp', 'sp'), may hold values from 1 to 160, 512 in all within a row
- out_weight: bfloat16 [4096, 2048], P('sp'), may hold values from -1 to 1
- residual: bfloat16 [5120, 2048], P(('grp', 'sp')), may hold values from -36 to 36
- norm_gain: float32 [2048], replicated, may hold values from 0.1 to 1.9
- expert_ids: int32 [5120, 8], P(('grp', 'sp')), may hold values from 0 to 31, all different within a row; in each aligned block of 160 rows (0 to 159, 160 to 319, ...) at most 64 rows name the same one
- gate_values: float32 [5120, 8], P(('grp', 'sp')), may hold values from 0.05 to 0.5
- up_gate_weight: bfloat16 [32, 2048, 1536], P(('grp', 'sp')), may hold values from -0.125 to 0.125
- down_weight: bfloat16 [32, 768, 2048], P(('grp', 'sp')), may hold values from -0.21875 to 0.21875
Outputs:
- attended: bfloat16 [5120, 2048], P(('grp', 'sp'))
- moe_out: bfloat16 [5120, 2048], P(('grp', 'sp'))
Inputs may be any that keep to these rules, and one draw needn't show every extreme that they name: Each group's 4 lengths sum to 512, and in every group one device has exactly 160. `expert_ids`: each slot names 8 different experts; among the 160 slots of one device no expert is named more than 64 times, and one expert is named exactly 64 times by the slots of some device.
All inputs are finite; a program needn't handle non-finite values.
Results may differ from a plain program's by a relative error of at most 0.02.
Values may be sent and summed in bfloat16 or wider, within the bound.
No kernel may reach another device: no remote copies, remote signals or barrier semaphores. Data moves between devices by JAX's collectives and lax.ppermute only.
A program may use at most 128 MiB of HBM per device.

v0:
```python
import functools
import math

import jax
import jax.numpy as jnp
from jax import lax
from jax.experimental import pallas as pl
from jax.experimental.pallas import tpu as pltpu
from jax.sharding import PartitionSpec as P


def partner_2(value, axis, bit):
    mask = 2**bit
    pairs = [(source, source ^ mask) for source in range(lax.axis_size(axis))]
    return lax.ppermute(value, axis, pairs)


def shift_z(value):
    groups = lax.axis_size("grp")
    return lax.ppermute(value, "grp", [(g, (g + 2) % groups) for g in range(groups)])


def swap_x(value):
    return partner_2(value, "grp", 0)


def swap_y(value):
    return partner_2(value, "sp", 1)


def swap_core(value):
    return partner_2(value, "sp", 0)


def after(value, *earlier):
    return lax.optimization_barrier((value, *earlier))[0]


def xor_group(value, mask):
    return lax.ppermute(value, "sp", [(s, s ^ mask) for s in range(lax.axis_size("sp"))])


def attend_kernel(index, mine_ref, query_ref, cache_ref, *refs):
    fresh_refs, (out_ref, keys, values, bias) = refs[:-4], refs[-4:]
    rows = query_ref.shape[0]
    cached, width = cache_ref.shape[0], cache_ref.shape[1] // 2
    keys[:cached, :] = cache_ref[:, :width]
    values[:cached, :] = cache_ref[:, width:]
    lengths = []
    for block, fresh_ref in enumerate(fresh_refs):
        places = pl.ds(cached + block * rows, rows)
        keys[places, :] = fresh_ref[:rows, :width]
        values[places, :] = fresh_ref[:rows, width:]
        note = fresh_ref[rows : rows + 16, :].astype(jnp.float32)
        lengths.append(note[:1, :1] * 256.0 + note[:1, width : width + 1])
    mine = mine_ref[0]
    offsets = []
    for block in range(len(fresh_refs)):
        offset = jnp.zeros((1, 1), jnp.float32)
        for other in range(len(fresh_refs)):
            before = (mine ^ other) < (mine ^ block)
            offset = offset + lengths[other] * before.astype(jnp.float32)
        offsets.append(offset)
    column = lax.broadcasted_iota(jnp.int32, (1, bias.shape[1]), 1)
    key_place = jnp.zeros((1, bias.shape[1]), jnp.float32)
    for block in range(len(fresh_refs)):
        within = (column - block * rows).astype(jnp.float32)
        place = jnp.where(within < lengths[block], within + offsets[block], 1e9)
        key_place = jnp.where(column >= block * rows, place, key_place)
    row_place = lax.broadcasted_iota(jnp.int32, bias.shape, 0).astype(jnp.float32) + offsets[index]
    bias[...] = jnp.where(key_place <= row_place, 0.0, -1e30)
    scale = math.log2(math.e) / math.sqrt(width)
    for head in range(query_ref.shape[1] // width):
        columns = pl.ds(head * width, width)
        scores = lax.dot_general(
            query_ref[:, columns],
            keys[...],
            (((1,), (1,)), ((), ())),
            preferred_element_type=jnp.float32,
        )
        old, new = scores[:, :cached] * scale, scores[:, cached:] * scale + bias[...]
        row_max = jnp.maximum(
            jnp.max(old, axis=1, keepdims=True), jnp.max(new, axis=1, keepdims=True)
        )
        old, new = jnp.exp2(old - row_max), jnp.exp2(new - row_max)
        totals = jnp.sum(old, axis=1, keepdims=True) + jnp.sum(new, axis=1, keepdims=True)
        result = jnp.dot(
            old.astype(jnp.bfloat16), values[:cached, :], preferred_element_type=jnp.float32
        ) + jnp.dot(
            new.astype(jnp.bfloat16), values[cached:, :], preferred_element_type=jnp.float32
        )
        out_ref[:, columns] = (result / totals).astype(jnp.bfloat16)


def attend_block(index, mine, query, cache_block, fresh):
    rows, columns = query.shape
    cached, width = cache_block.shape[0], cache_block.shape[1] // 2
    new = rows * len(fresh)
    inside = pl.BlockSpec(memory_space=pltpu.VMEM)
    return pl.pallas_call(
        functools.partial(attend_kernel, index),
        out_shape=jax.ShapeDtypeStruct((rows, columns), jnp.bfloat16),
        in_specs=[pl.BlockSpec(memory_space=pltpu.SMEM)] + [inside] * (2 + len(fresh)),
        out_specs=inside,
        scratch_shapes=[
            pltpu.VMEM((cached + new, width), jnp.bfloat16),
            pltpu.VMEM((cached + new, width), jnp.bfloat16),
            pltpu.VMEM((rows, new), jnp.float32),
        ],
        compiler_params=pltpu.CompilerParams(vmem_limit_bytes=40 * 2**20),
        cost_estimate=pl.CostEstimate(
            flops=4 * rows * columns * (cached + new),
            bytes_accessed=4 * (rows * columns + (cached + new) * width),
            transcendentals=rows * columns // width * (cached + new),
        ),
    )(mine, query, cache_block, *fresh)


def norm_kernel(
    length_ref,
    own_ref,
    core_ref,
    far_ref,
    residual_ref,
    gain_ref,
    attended_ref,
    packed_ref,
):
    attn_sum = (
        own_ref[...].astype(jnp.float32)
        + core_ref[...].astype(jnp.float32)
        + far_ref[...].astype(jnp.float32)
    )
    live = lax.broadcasted_iota(jnp.int32, attn_sum.shape, 0) < length_ref[0]
    attended_ref[...] = jnp.where(live, attn_sum, 0.0).astype(jnp.bfloat16)
    mixed = residual_ref[...].astype(jnp.float32) + attn_sum
    scale = lax.rsqrt(jnp.mean(mixed * mixed, axis=1, keepdims=True) + 1e-06)
    normed = (mixed * scale * gain_ref[...]).astype(jnp.bfloat16)
    rows, half = packed_ref.shape[0] // 2, packed_ref.shape[1]
    packed_ref[:rows, :] = normed[:, :half]
    packed_ref[rows:, :] = normed[:, half:]


def normalize(length, own, core, far, residual, gain):
    rows, width = own.shape
    packed = jax.ShapeDtypeStruct((2 * rows, width // 2), jnp.bfloat16)
    inside = pl.BlockSpec(memory_space=pltpu.VMEM)
    return pl.pallas_call(
        norm_kernel,
        out_shape=(jax.ShapeDtypeStruct((rows, width), jnp.bfloat16), packed),
        in_specs=[pl.BlockSpec(memory_space=pltpu.SMEM)] + [inside] * 5,
        out_specs=(inside, inside),
        compiler_params=pltpu.CompilerParams(vmem_limit_bytes=40 * 2**20),
        cost_estimate=pl.CostEstimate(
            flops=10 * rows * width, bytes_accessed=12 * rows * width, transcendentals=rows
        ),
    )(length, own, core, far, residual, gain)


def pick_kernel(capacity, place_ref, *refs):
    blocks, _, rows = place_ref.shape
    own_ref, sibling_ref = refs[-2:]
    half = own_ref.shape[1] // 2
    slot = lax.broadcasted_iota(jnp.int32, (capacity, rows), 0)
    for block in range(blocks):
        pick = jnp.concatenate(
            [(place_ref[block, pl.ds(core, 1), :] == slot) for core in range(2)], axis=0
        )
        pick = jnp.where(pick, 1.0, 0.0).astype(jnp.bfloat16)
        level, spot = block // 4, block % 4
        for side in range(2):
            if spot < 3:
                source = refs[5 * level + spot][pl.ds(side * rows, rows), :]
            else:
                source = refs[5 * level + 3 + side][...]
            chosen = jnp.dot(pick, source, preferred_element_type=jnp.float32)
            chosen = chosen.astype(jnp.bfloat16)
            inner = pl.ds(block * capacity, capacity), pl.ds(side * half, half)
            own_ref[inner] = chosen[:capacity]
            sibling_ref[inner] = chosen[capacity:]


def pick_rows(capacity, place, gathered):
    blocks, _, rows = place.shape
    half = gathered[0].shape[1]
    shape = jax.ShapeDtypeStruct((blocks * capacity, 2 * half), jnp.bfloat16)
    return pl.pallas_call(
        functools.partial(pick_kernel, capacity),
        out_shape=(shape, shape),
        compiler_params=pltpu.CompilerParams(vmem_limit_bytes=48 * 2**20),
        cost_estimate=pl.CostEstimate(
            flops=8 * blocks * capacity * rows * half,
            bytes_accessed=4 * blocks * (rows + 2 * capacity) * half,
            transcendentals=0,
        ),
    )(place, *gathered)


def combine_kernel(place_ref, gate_ref, own_ref, other_ref, *out_refs):
    blocks, _, rows = place_ref.shape
    capacity = own_ref.shape[0] // blocks
    half = own_ref.shape[1] // 2
    slot = lax.broadcasted_iota(jnp.int32, (capacity, rows), 0)
    for block in range(blocks):
        weight = jnp.concatenate(
            [
                jnp.where(
                    place_ref[block, pl.ds(core, 1), :] == slot,
                    gate_ref[block, pl.ds(core, 1), :],
                    0.0,
                )
                for core in range(2)
            ],
            axis=0,
        )
        weight = weight.T.astype(jnp.bfloat16)
        level, (far_x, far_y) = block // 4, (block // 2 % 2, block % 2)
        for side in range(2):
            inner = pl.ds(block * capacity, capacity), pl.ds(side * half, half)
            both = jnp.concatenate([own_ref[inner], other_ref[inner]], axis=0)
            share = jnp.dot(weight, both, preferred_element_type=jnp.float32).astype(jnp.bfloat16)
            sent, place = (far_x, far_y) if side else (far_y, far_x)
            if sent:
                out_refs[6 * level + 3 * side + 2][pl.ds(place * rows, rows), :] = share
            else:
                out_refs[6 * level + 3 * side + place][...] = share


def combine_rows(place, gate, own, other):
    blocks, _, rows = place.shape
    half = own.shape[1] // 2
    kept = jax.ShapeDtypeStruct((rows, half), jnp.bfloat16)
    sent = jax.ShapeDtypeStruct((2 * rows, half), jnp.bfloat16)
    return pl.pallas_call(
        combine_kernel,
        out_shape=[kept, kept, sent] * (blocks // 2),
        compiler_params=pltpu.CompilerParams(vmem_limit_bytes=48 * 2**20),
        cost_estimate=pl.CostEstimate(
            flops=8 * own.shape[0] * rows * half,
            bytes_accessed=4 * (blocks * rows + 2 * own.shape[0]) * half,
            transcendentals=0,
        ),
    )(place, gate, own, other)


def routing_start(own_live, expert_ids, gate_values, earlier):
    live_ids = jnp.where(own_live[:, None], expert_ids, -1).astype(jnp.float32)
    routing = after(jnp.concatenate([live_ids, gate_values], axis=1).T, earlier)
    groups = lax.axis_size("grp")
    lines = [routing]
    for hop in range(2, groups, 2):
        lines.append(
            lax.ppermute(routing, "grp", [(g, (g + hop) % groups) for g in range(groups)])
        )
    return jnp.stack(lines)


def routing_pair(routing, swap):
    return jnp.stack([routing, swap(routing)], axis=routing.ndim - 2)


def selections(routing, top_count):
    mine = lax.axis_index(("grp", "sp"))
    depth, rows = routing.shape[0], routing.shape[-1]
    routing = routing.reshape(-1, 2 * top_count, rows)
    ids, gates = routing[:, :top_count].astype(jnp.int32), routing[:, top_count:]
    experts = jnp.stack([mine, mine ^ 1])
    chosen = ids[:, None] == experts[None, :, None, None]
    wanted = jnp.any(chosen, axis=2)
    gate = jnp.sum(jnp.where(chosen, gates[:, None], 0.0), axis=2)
    order = jnp.arange(rows)
    earlier = (order[:, None] < order[None, :]).astype(jnp.bfloat16)
    place = jnp.einsum(
        "bcr,rt->bct", wanted.astype(jnp.bfloat16), earlier, preferred_element_type=jnp.float32
    ).astype(jnp.int32)
    return jnp.where(wanted, place, -1), gate


def run_expert(rows, up_gate_weight, down_weight):
    hidden_width = down_weight.shape[1]
    projected = jnp.dot(rows, up_gate_weight[0], preferred_element_type=jnp.float32)
    hidden = (jax.nn.silu(projected[:, :hidden_width]) * projected[:, hidden_width:]).astype(
        jnp.bfloat16
    )
    return jnp.dot(hidden, down_weight[0], preferred_element_type=jnp.float32).astype(jnp.bfloat16)


def experts_by_gather(packed, place, gate, capacity, up_gate_weight, down_weight):
    depth = lax.axis_size("grp") // 2
    per_level = place.shape[0] // depth
    rows = packed.shape[0] // 2
    lines, beside_x, beside_y, diagonal = [packed], [], [], []

    def cross(level, earlier):
        first_x, second_y = beside_x[level][:rows], beside_y[level][rows:]
        if earlier is not None:
            first_x, second_y = after(first_x, earlier), after(second_y, earlier)
        diagonal.append((swap_y(first_x), swap_x(second_y)))

    for level in range(depth):
        line = lines[level]
        if level == 2:
            cross(0, line)
            cross(1, line)
            line = after(line, *diagonal[0], *diagonal[1])
        elif level > 2:
            line = after(line, beside_x[level - 1], beside_y[level - 1])
        beside_x.append(swap_x(line))
        beside_y.append(swap_y(line))
        if level + 1 < depth:
            line = lines[level]
            if level:
                line = after(line, beside_x[level - 1], beside_y[level - 1])
            lines.append(shift_z(line))
    for level in range(len(diagonal), depth):
        cross(level, None)
    kept, sent, back, joined = {}, {}, {}, {}

    def send_back(level, *earlier):
        first_sent, second_sent = sent[level]
        if earlier:
            first_sent, second_sent = after(first_sent, *earlier), after(second_sent, *earlier)
        back[level] = swap_y(first_sent), swap_x(second_sent)

    def join(level):
        first, first_x, second, second_y = kept[level]
        first_back, second_back = back[level]
        first, first_x = first + first_back[:rows], first_x + first_back[rows:]
        second, second_y = second + second_back[:rows], second_y + second_back[rows:]
        joined[level] = first, second, swap_x(first_x), swap_y(second_y)

    for start in range(0, depth, 2):
        levels = range(start, min(start + 2, depth))
        gathered = []
        for level in levels:
            gathered += [lines[level], beside_y[level], beside_x[level], *diagonal[level]]
        ahead, last = levels[-1] + 1, levels[-1] + 2
        if last < depth:
            gathered[0] = after(gathered[0], lines[last])
        if start:
            gathered[0] = after(gathered[0], kept[start - 1][0])
        blocks = slice(start * per_level, (start + len(levels)) * per_level)
        own, sibling = pick_rows(capacity, place[blocks], gathered)
        if last < depth:
            sibling = after(sibling, beside_x[ahead], beside_y[ahead])
        other = swap_core(sibling)
        other_result = run_expert(other, up_gate_weight, down_weight)
        if last < depth:
            own = after(own, beside_x[last], beside_y[last])
        if start:
            back[start - 1] = tuple(after(part, other_result) for part in back[start - 1])
            join(start - 1)
            own = after(own, *back[start - 1])
        own_result = run_expert(own, up_gate_weight, down_weight)
        other_result = swap_core(other_result)
        if last < depth:
            own_result = after(own_result, *diagonal[ahead])
        if start:
            own_result = after(own_result, *joined[start - 1])
        parts = combine_rows(place[blocks], gate[blocks], own_result, other_result)
        for index, level in enumerate(levels):
            first, first_x, first_sent, second, second_y, second_sent = parts[
                6 * index : 6 * index + 6
            ]
            kept[level] = first, first_x, second, second_y
            sent[level] = first_sent, second_sent
        levels = [level for level in levels if level]
        for level in levels:
            send_back(level, *back.get(level - 1, ()))
        if ahead < depth:
            levels = levels[:-1]
        for level in levels:
            join(level)
    send_back(0, *back.get(depth - 1, ()))
    join(0)
    shares = {}
    for level in range(depth):
        first, second, first_far, second_far = joined[level]
        shares[level] = first + first_far, second + second_far
    first, second = shares[0]
    if depth > 1:
        total = jnp.concatenate(shares[1], axis=0)
        for level in range(2, depth):
            total = jnp.concatenate(shares[level], axis=0) + shift_z(total)
        total = shift_z(total)
        first, second = first + total[:rows], second + total[rows:]
    return jnp.concatenate([first, second], axis=1)


def per_device_pairs(
    queries,
    fresh_key_values,
    cache,
    lengths,
    out_weight,
    residual,
    norm_gain,
    expert_ids,
    gate_values,
    up_gate_weight,
    down_weight,
):
    seq_devices = lax.axis_size("sp")
    mine = lax.axis_index("sp")
    slot_rows = queries.shape[0]
    width = cache.shape[-1] // 2
    head_columns = queries.shape[1] // seq_devices
    top_count = expert_ids.shape[1]
    experts = up_gate_weight.shape[0] * lax.axis_size("grp") * seq_devices
    capacity = max(2, 8 * slot_rows * top_count // (5 * experts))
    own_length = lengths[0, 0]
    own_live = jnp.arange(slot_rows, dtype=jnp.int32) < own_length

    def key_values_for(target):
        keys = lax.dynamic_slice(fresh_key_values, (0, target * width), (slot_rows, width))
        values = lax.dynamic_slice(
            fresh_key_values, (0, (seq_devices + target) * width), (slot_rows, width)
        )
        lane = jnp.arange(2 * width, dtype=jnp.int32)[None, :]
        note = jnp.where(lane < width, own_length // 256, own_length % 256)
        note = jnp.broadcast_to(note, (16, 2 * width)).astype(jnp.bfloat16)
        return jnp.concatenate([jnp.concatenate([keys, values], axis=1), note], axis=0)

    def queries_for(target):
        return lax.dynamic_slice(queries, (0, target * head_columns), (slot_rows, head_columns))

    masks = range(1, seq_devices)
    fresh = [key_values_for(mine)] + [xor_group(key_values_for(mine ^ m), m) for m in masks]
    query_blocks = [queries_for(mine)] + [xor_group(queries_for(mine ^ m), m) for m in masks]
    cache_block = cache[0, 0]

    def share_of(block, query):
        heads = attend_block(block, mine[None], query, cache_block, fresh)
        return jnp.dot(heads, out_weight, preferred_element_type=jnp.float32).astype(jnp.bfloat16)

    own = share_of(0, query_blocks[0])
    routing = routing_start(own_live, expert_ids, gate_values, own)
    far_core = share_of(3, after(query_blocks[3], query_blocks[2], own, routing))
    routing = routing_pair(routing, swap_x)
    far = share_of(2, after(query_blocks[2], routing)) + swap_core(far_core)
    near = share_of(1, after(query_blocks[1], far))
    far = swap_y(far)
    attended, packed = normalize(
        lengths[0], own, swap_core(after(near, far)), far, residual, norm_gain[None, :]
    )
    routing = routing_pair(after(routing, packed), swap_y)
    place, gate = selections(routing, top_count)
    moe_out = experts_by_gather(packed, place, gate, capacity, up_gate_weight, down_weight)
    return (attended, moe_out)


def per_device(
    queries,
    fresh_key_values,
    cache,
    lengths,
    out_weight,
    residual,
    norm_gain,
    expert_ids,
    gate_values,
    up_gate_weight,
    down_weight,
):
    seq_devices = lax.axis_size("sp")
    slot_rows = queries.shape[0]
    head_width = cache.shape[-1] // 2
    model_width = residual.shape[1]
    kv_heads = fresh_key_values.shape[1] // (2 * head_width)
    repeat = seq_devices // kv_heads
    keys_new = fresh_key_values[:, : kv_heads * head_width].reshape(
        slot_rows, kv_heads, 1, head_width
    )
    values_new = fresh_key_values[:, kv_heads * head_width :].reshape(
        slot_rows, kv_heads, 1, head_width
    )
    paired = jnp.concatenate([keys_new, values_new], axis=3)
    spread = jnp.broadcast_to(paired, (slot_rows, kv_heads, repeat, 2 * head_width)).reshape(
        slot_rows, seq_devices * 2 * head_width
    )
    all_lengths = lax.all_gather(lengths, "sp", axis=1, tiled=True)
    queries_by_head, head_kv = (
        lax.all_to_all(queries, "sp", split_axis=1, concat_axis=0, tiled=True),
        lax.all_to_all(spread, "sp", split_axis=1, concat_axis=0, tiled=True),
    )
    cache_block = cache[0, 0]
    my_index = lax.axis_index("sp")
    for bit_pos in range(repeat.bit_length() - 1):
        partner = partner_2(cache_block, "sp", bit_pos)
        is_upper = my_index // 2**bit_pos % 2 == 1
        cache_block = jnp.where(
            is_upper,
            jnp.concatenate([partner, cache_block], axis=0),
            jnp.concatenate([cache_block, partner], axis=0),
        )
    stretch_lens = all_lengths[0]
    offsets = jnp.cumsum(stretch_lens) - stretch_lens
    rows_of_group = queries_by_head.shape[0]
    slot_ids = jnp.arange(rows_of_group, dtype=jnp.int32)
    source = slot_ids // slot_rows
    within = slot_ids % slot_rows
    from_device = source[:, None] == jnp.arange(seq_devices, dtype=jnp.int32)[None, :]
    is_live = within < jnp.sum(jnp.where(from_device, stretch_lens[None, :], 0), axis=1)
    position = within + jnp.sum(jnp.where(from_device, offsets[None, :], 0), axis=1)
    per_dev = queries_by_head.shape[1] // head_width
    cache_len = cache_block.shape[0]
    key_all = jnp.concatenate([cache_block[:, :head_width], head_kv[:, :head_width]], axis=0)
    value_all = jnp.concatenate([cache_block[:, head_width:], head_kv[:, head_width:]], axis=0)
    block_count = 2 if rows_of_group % 2 == 0 and rows_of_group >= 1024 else 1
    block_rows = rows_of_group // block_count

    def attend(parts):
        query_block, place_block = parts
        scores = jnp.einsum(
            "rhd,kd->hrk", query_block, key_all, preferred_element_type=jnp.float32
        ) / math.sqrt(head_width)
        allowed = jnp.concatenate(
            [
                jnp.ones((block_rows, cache_len), dtype=bool),
                is_live[None, :] & (position[None, :] <= place_block[:, None]),
            ],
            axis=1,
        )
        scores = jnp.where(allowed[None], scores, -jnp.inf)
        row_max = jnp.max(scores, axis=-1, keepdims=True)
        weights = jnp.exp(scores - row_max)
        totals = jnp.sum(weights, axis=-1, keepdims=True)
        result = (
            jnp.einsum(
                "hrk,kd->hrd",
                weights.astype(jnp.bfloat16),
                value_all,
                preferred_element_type=jnp.float32,
            )
            / totals
        )
        return (
            result.astype(jnp.bfloat16).transpose(1, 0, 2).reshape(block_rows, per_dev * head_width)
        )

    attn_heads = lax.map(
        attend,
        (
            queries_by_head.reshape(block_count, block_rows, per_dev, head_width),
            position.reshape(block_count, block_rows),
        ),
    ).reshape(rows_of_group, per_dev * head_width)
    attn_sum = lax.psum_scatter(
        jnp.dot(attn_heads, out_weight, preferred_element_type=jnp.float32).astype(jnp.bfloat16),
        "sp",
        scatter_dimension=0,
        tiled=True,
    ).astype(jnp.float32)
    own_live = jnp.arange(slot_rows, dtype=jnp.int32) < lengths[0, 0]
    attended = jnp.where(own_live[:, None], attn_sum, 0.0).astype(jnp.bfloat16)
    mixed_rows = residual.astype(jnp.float32) + attn_sum
    normed = (
        mixed_rows
        * lax.rsqrt(jnp.mean(mixed_rows * mixed_rows, axis=-1, keepdims=True) + 1e-06)
        * norm_gain
    ).astype(jnp.bfloat16)
    group_count = lax.axis_size("grp")
    experts = up_gate_weight.shape[0] * group_count * seq_devices
    top_count = expert_ids.shape[1]
    capacity = max(2, 8 * slot_rows * top_count // (5 * experts))
    hidden_width = down_weight.shape[1]
    choose = expert_ids[:, :, None] == jnp.arange(experts, dtype=jnp.int32)[None, None, :]
    routed = (jnp.any(choose, axis=1) & own_live[:, None]).astype(jnp.float32)
    earlier = (jnp.arange(slot_rows)[:, None] > jnp.arange(slot_rows)[None, :]).astype(jnp.float32)
    prefix = jnp.dot(earlier, routed, precision=lax.Precision.HIGHEST)
    slot_in = jnp.sum(jnp.where(choose, prefix[:, None, :], 0.0), axis=2).astype(jnp.int32)
    dump_slot = experts * capacity
    target = jnp.where(own_live[:, None], expert_ids * capacity + slot_in, dump_slot)
    source_rows = (
        jnp.full((dump_slot + 1,), slot_rows, jnp.int32)
        .at[target.reshape(-1)]
        .set(jnp.repeat(jnp.arange(slot_rows, dtype=jnp.int32), top_count))[:dump_slot]
    )
    padded = jnp.concatenate([normed, jnp.zeros((1, model_width), jnp.bfloat16)], axis=0)
    outgoing = padded[source_rows].reshape(experts, capacity, model_width)
    received = lax.all_to_all(outgoing, ("grp", "sp"), split_axis=0, concat_axis=0, tiled=True)
    flat_rows = received.reshape(-1, model_width)
    projected = jnp.dot(flat_rows, up_gate_weight[0], preferred_element_type=jnp.float32)
    hidden = (jax.nn.silu(projected[:, :hidden_width]) * projected[:, hidden_width:]).astype(
        jnp.bfloat16
    )
    returned = lax.all_to_all(
        jnp.dot(hidden, down_weight[0], preferred_element_type=jnp.float32)
        .astype(jnp.bfloat16)
        .reshape(received.shape),
        ("grp", "sp"),
        split_axis=0,
        concat_axis=0,
        tiled=True,
    )
    back_rows = jnp.concatenate(
        [returned.reshape(dump_slot, model_width), jnp.zeros((1, model_width), jnp.bfloat16)],
        axis=0,
    )
    picked = back_rows[target]
    combined = jnp.sum(gate_values[:, :, None] * picked.astype(jnp.float32), axis=1)
    moe_out = jnp.where(own_live[:, None], combined, 0.0).astype(jnp.bfloat16)
    return (attended, moe_out)


def solution(mesh):
    in_specs = (
        P(("grp", "sp"), None),
        P(("grp", "sp"), None),
        P("grp", "sp", None, None),
        P("grp", "sp"),
        P("sp", None),
        P(("grp", "sp"), None),
        P(),
        P(("grp", "sp"), None),
        P(("grp", "sp"), None),
        P(("grp", "sp"), None, None),
        P(("grp", "sp"), None, None),
    )
    out_specs = (P(("grp", "sp"), None), P(("grp", "sp"), None))
    groups, seq_devices = mesh.shape["grp"], mesh.shape["sp"]

    def run(*args):
        kv_heads = args[1].shape[1] // args[2].shape[-1]
        experts, top_count = args[9].shape[0], args[7].shape[1]
        pairs = seq_devices == kv_heads == 4 and groups % 2 == 0 and experts <= 4 * top_count
        return mapped(per_device_pairs if pairs else per_device)(*args)

    def mapped(body):
        return jax.shard_map(
            body, mesh=mesh, in_specs=in_specs, out_specs=out_specs, check_vma=False
        )

    return run
```

profile of v0, /device:TPU:0, one launch (start us, length us, event | category | flops | bytes accessed | tf_op | source)
XLA Modules:
  0.0 279.4 jit_solution(12597092716017432022)
XLA Ops:
  3.8 2.5 collective-permute-start.1
  8.0 1.7 collective-permute-start.9
  11.7 4.6 %shard_map.122 = bf16[160,1024]{1,0:T(8,128)(2,1)S(1)} custom-call(s32[1]{0:T(128)} %bitcast.1.mine_ref, bf16[160,1024]{1,0:T(8,128)(2,1)S(1)} %get-tuple-element.126.query_ref, bf16[512,256]{1,0:T(8,128)(2,1)S(1)} %bitcast.71, bf16[176,256]{1,0:T(8,128)(2,1)S(1)} %get-tuple-element.149.refs_0_, bf16[176,256]{1,0:T(8,128)(2,1)} %collective-permute-done.refs_1_, ...), custom_call_target="tpu_custom_call" | custom-call | flops 754974720 | bytes 1245184 | tf_op jit(solution)/shard_map/pallas_call | solution.py:100
  17.2 3.7 %collective-permute-start.7 = (f32[16,160]{1,0:T(8,128)S(1)}, f32[16,160]{1,0:T(8,128)S(1)}, u32[]{:S(2)}, u32[]{:S(2)}) collective-permute-start(f32[16,160]{1,0:T(8,128)S(1)} %maximum_bitcast_fusion), channel_id=1, source_target_pairs={{0,24},{4,28},{8,0},{12,4},{16,8},{20,12},{24,16},{28,20},{1,25},{... | collective-permute-start | bytes 30728 | tf_op jit(solution)/shard_map/ppermute | solution.py:253
  22.3 3.2 %collective-permute-done.6 = f32[16,160]{1,0:T(8,128)S(1)} collective-permute-done((f32[16,160]{1,0:T(8,128)S(1)}, f32[16,160]{1,0:T(8,128)S(1)}, u32[]{:S(2)}, u32[]{:S(2)}) %collective-permute-start.6) | collective-permute-done | bytes 10272 | tf_op jit(solution)/shard_map/ppermute | solution.py:253
  26.6 4.6 %shard_map.124 = bf16[160,1024]{1,0:T(8,128)(2,1)S(1)} custom-call(s32[1]{0:T(128)} %bitcast.1.mine_ref, bf16[160,1024]{1,0:T(8,128)(2,1)S(1)} %collective-permute-done.9.query_ref, bf16[512,256]{1,0:T(8,128)(2,1)S(1)} %bitcast.72, bf16[176,256]{1,0:T(8,128)(2,1)S(1)} %get-tuple-element.149.refs_0_, bf16[176,256]{1,0:T(8,128)(2,1)} %collective-permute-done.refs_1_, ...), custom_call_target="tpu_custom_call" | custom-call | flops 754974720 | bytes 1245184 | tf_op jit(solution)/shard_map/pallas_call | solution.py:100
  33.8 2.8 collective-permute-done.8
  37.3 4.6 %shard_map.123 = bf16[160,1024]{1,0:T(8,128)(2,1)S(1)} custom-call(s32[1]{0:T(128)} %bitcast.1.mine_ref, bf16[160,1024]{1,0:T(8,128)(2,1)S(1)} %collective-permute-done.4.query_ref, bf16[512,256]{1,0:T(8,128)(2,1)S(1)} %bitcast.73, bf16[176,256]{1,0:T(8,128)(2,1)S(1)} %get-tuple-element.149.refs_0_, bf16[176,256]{1,0:T(8,128)(2,1)} %collective-permute-done.refs_1_, ...), custom_call_target="tpu_custom_call" | custom-call | flops 754974720 | bytes 1245184 | tf_op jit(solution)/shard_map/pallas_call | solution.py:100
  44.3 4.6 %shard_map.125 = bf16[160,1024]{1,0:T(8,128)(2,1)S(1)} custom-call(s32[1]{0:T(128)} %bitcast.1.mine_ref, bf16[160,1024]{1,0:T(8,128)(2,1)S(1)} %collective-permute-done.3.query_ref, bf16[512,256]{1,0:T(8,128)(2,1)S(1)} %bitcast.74, bf16[176,256]{1,0:T(8,128)(2,1)S(1)} %get-tuple-element.149.refs_0_, bf16[176,256]{1,0:T(8,128)(2,1)} %collective-permute-done.refs_1_, ...), custom_call_target="tpu_custom_call" | custom-call | flops 754974720 | bytes 1245184 | tf_op jit(solution)/shard_map/pallas_call | solution.py:100
  50.0 9.1 %collective-permute-done.11.far_ref = bf16[160,2048]{1,0:T(8,128)(2,1)S(1)} collective-permute-done((bf16[160,2048]{1,0:T(8,128)(2,1)S(1)}, bf16[160,2048]{1,0:T(8,128)(2,1)S(1)}, u32[]{:S(2)}, u32[]{:S(2)}) %collective-permute-start.11) | collective-permute-done | bytes 655392 | tf_op jit(solution)/shard_map/ppermute | solution.py:15
  59.1 2.1 collective-permute-done.12.core_ref
  67.4 13.8 %collective-permute-done.14.refs_5_ = bf16[320,1024]{1,0:T(8,128)(2,1)} collective-permute-done((bf16[320,1024]{1,0:T(8,128)(2,1)S(1)}, bf16[320,1024]{1,0:T(8,128)(2,1)}, u32[]{:S(2)}, u32[]{:S(2)}) %collective-permute-start.14) | collective-permute-done | bytes 655392 | tf_op jit(solution)/shard_map/ppermute | solution.py:20
  81.4 1.6 collective-permute-start.17
  85.6 15.9 %collective-permute-done.13 = f32[4,2,16,160]{3,2,1,0:T(8,128)S(1)} collective-permute-done((f32[4,2,16,160]{3,2,1,0:T(8,128)S(1)}, f32[4,2,16,160]{3,2,1,0:T(8,128)S(1)}, u32[]{:S(2)}, u32[]{:S(2)}) %collective-permute-start.13) | collective-permute-done | bytes 81952 | tf_op jit(solution)/shard_map/ppermute | solution.py:15
  103.5 1.6 collective-permute-start.21
  111.4 2.7 collective-permute-done.21.refs_3_
  115.4 2.3 collective-permute-done.23.refs_8_
  117.7 2.1 collective-permute-done.24.refs_9_
  121.6 3.8 %collective-permute-done.20.refs_5_ = bf16[320,1024]{1,0:T(8,128)(2,1)S(1)} collective-permute-done((bf16[320,1024]{1,0:T(8,128)(2,1)}, bf16[320,1024]{1,0:T(8,128)(2,1)S(1)}, u32[]{:S(2)}, u32[]{:S(2)}) %collective-permute-start.20) | collective-permute-done | bytes 655392 | tf_op jit(solution)/shard_map/ppermute | solution.py:20
  125.4 5.1 %shard_map.127 = (bf16[512,2048]{1,0:T(8,128)(2,1)}, bf16[512,2048]{1,0:T(8,128)(2,1)}) custom-call(s32[8,2,160]{2,1,0:T(2,128)S(1)} %get-tuple-element.145.place_ref, bf16[320,1024]{1,0:T(8,128)(2,1)S(1)} %copy-done.2, bf16[320,1024]{1,0:T(8,128)(2,1)} %collective-permute-done.16.refs_1_, bf16[320,1024]{1,0:T(8,128)(2,1)} %collective-permute-done.15.refs_2_, ...), custom_call_target="tpu_custom_call" | custom-call | flops 671088640 | bytes 9437184 | tf_op jit(solution)/shard_map/pallas_call | solution.py:187
  130.5 2.5 collective-permute-done.25.refs_2_
  135.2 2.1 collective-permute-done.31
  137.3 5.5 %fusion.4 = f32[512,1536]{1,0:T(8,128)S(1)} fusion(bf16[512,2048]{1,0:T(8,128)(2,1)S(1)} %collective-permute-done.31, bf16[1,2048,1536]{2,1,0:T(8,128)(2,1)} %param.20), kind=kOutput, calls=%fused_computation.4 | convolution fusion | flops 3221225472 | bytes 11534336 | tf_op jit(solution)/shard_map/dot_general | solution.py:281
  142.9 1.9 fusion.19
  147.6 2.9 %collective-permute-done.27.refs_7_ = bf16[320,1024]{1,0:T(8,128)(2,1)S(1)} collective-permute-done((bf16[320,1024]{1,0:T(8,128)(2,1)S(1)}, bf16[320,1024]{1,0:T(8,128)(2,1)S(1)}, u32[]{:S(2)}, u32[]{:S(2)}) %collective-permute-start.27) | collective-permute-done | bytes 655392 | tf_op jit(solution)/shard_map/ppermute | solution.py:15
  154.0 5.5 %fusion.6 = f32[512,1536]{1,0:T(8,128)S(1)} fusion(bf16[512,2048]{1,0:T(8,128)(2,1)S(1)} %copy-done.12, bf16[1,2048,1536]{2,1,0:T(8,128)(2,1)} %param.20), kind=kOutput, calls=%fused_computation.6 | convolution fusion | flops 3221225472 | bytes 11534336 | tf_op jit(solution)/shard_map/dot_general | solution.py:281
  159.5 3.2 %fusion.16.own_ref = bf16[512,2048]{1,0:T(8,128)(2,1)} fusion(bf16[1,768,2048]{2,1,0:T(8,128)(2,1)S(1)} %copy-done, f32[512,1536]{1,0:T(8,128)S(1)} %fusion.6), kind=kOutput, calls=%fused_computation.16 | convolution fusion | flops 1614020608 | bytes 8388608 | tf_op jit(solution)/shard_map/dot_general | solution.py:285
  164.1 3.8 %shard_map.128 = (bf16[160,1024]{1,0:T(8,128)(2,1)S(1)}, bf16[160,1024]{1,0:T(8,128)(2,1)S(1)}, bf16[320,1024]{1,0:T(8,128)(2,1)S(1)}, bf16[160,1024]{1,0:T(8,12...) custom-call(s32[8,2,160]{2,1,0:T(2,128)S(1)} %get-tuple-element.145., ...), custom_call_target="tpu_custom_call" | custom-call | flops 671088640 | bytes 9437184 | tf_op jit(solution)/shard_map/pallas_call | solution.py:234
  167.9 4.3 %shard_map.129 = (bf16[512,2048]{1,0:T(8,128)(2,1)}, bf16[512,2048]{1,0:T(8,128)(2,1)}) custom-call(s32[8,2,160]{2,1,0:T(2,128)S(1)} %get-tuple-element.144.place_ref, bf16[320,1024]{1,0:T(8,128)(2,1)} %collective-permute-done.17.refs_0_, bf16[320,1024]{1,0:T(8,128)(2,1)S(1)} %collective-permute-done.26.refs_1_, ...), custom_call_target="tpu_custom_call" | custom-call | flops 671088640 | bytes 9437184 | tf_op jit(solution)/shard_map/pallas_call | solution.py:187
  174.1 2.5 collective-permute-done.36
  176.6 5.7 %fusion.2 = f32[512,1536]{1,0:T(8,128)S(1)} fusion(bf16[512,2048]{1,0:T(8,128)(2,1)S(1)} %collective-permute-done.36, bf16[1,2048,1536]{2,1,0:T(8,128)(2,1)} %param.20), kind=kOutput, calls=%fused_computation.2 | convolution fusion | flops 3221225472 | bytes 11534336 | tf_op jit(solution)/shard_map/dot_general | solution.py:281
  182.3 1.8 fusion.22
  184.4 4.9 %collective-permute-done.37 = bf16[320,1024]{1,0:T(8,128)(2,1)S(1)} collective-permute-done((bf16[320,1024]{1,0:T(8,128)(2,1)S(1)}, bf16[320,1024]{1,0:T(8,128)(2,1)S(1)}, u32[]{:S(2)}, u32[]{:S(2)}) %collective-permute-start.37) | collective-permute-done | bytes 655392 | tf_op jit(solution)/shard_map/ppermute | solution.py:15
  191.4 5.5 %fusion = f32[512,1536]{1,0:T(8,128)S(1)} fusion(bf16[512,2048]{1,0:T(8,128)(2,1)S(1)} %copy-done.13, bf16[1,2048,1536]{2,1,0:T(8,128)(2,1)} %param.20), kind=kOutput, calls=%fused_computation | convolution fusion | flops 3221225472 | bytes 11534336 | tf_op jit(solution)/shard_map/dot_general | solution.py:281
  197.0 3.2 %fusion.25.own_ref = bf16[512,2048]{1,0:T(8,128)(2,1)} fusion(bf16[1,768,2048]{2,1,0:T(8,128)(2,1)S(1)} %copy-done, f32[512,1536]{1,0:T(8,128)S(1)} %fusion), kind=kOutput, calls=%fused_computation.19 | convolution fusion | flops 1614020608 | bytes 8388608 | tf_op jit(solution)/shard_map/dot_general | solution.py:285
  201.6 3.8 %shard_map.130 = (bf16[160,1024]{1,0:T(8,128)(2,1)S(1)}, bf16[160,1024]{1,0:T(8,128)(2,1)S(1)}, bf16[320,1024]{1,0:T(8,128)(2,1)S(1)}, bf16[160,1024]{1,0:T(8,12...) custom-call(s32[8,2,160]{2,1,0:T(2,128)S(1)} %get-tuple-element.144., ...), custom_call_target="tpu_custom_call" | custom-call | flops 671088640 | bytes 9437184 | tf_op jit(solution)/shard_map/pallas_call | solution.py:234
  207.7 13.6 %collective-permute-done.42 = bf16[320,1024]{1,0:T(8,128)(2,1)S(1)} collective-permute-done((bf16[320,1024]{1,0:T(8,128)(2,1)S(1)}, bf16[320,1024]{1,0:T(8,128)(2,1)S(1)}, u32[]{:S(2)}, u32[]{:S(2)}) %collective-permute-start.42) | collective-permute-done | bytes 655392 | tf_op jit(solution)/shard_map/ppermute | solution.py:15
  224.7 1.6 collective-permute-start.51
  227.2 4.8 %collective-permute-done.50 = bf16[160,1024]{1,0:T(8,128)(2,1)S(1)} collective-permute-done((bf16[160,1024]{1,0:T(8,128)(2,1)S(1)}, bf16[160,1024]{1,0:T(8,128)(2,1)S(1)}, u32[]{:S(2)}, u32[]{:S(2)}) %collective-permute-start.50) | collective-permute-done | bytes 327712 | tf_op jit(solution)/shard_map/ppermute | solution.py:15
  232.1 12.1 %collective-permute-done.49 = bf16[160,1024]{1,0:T(8,128)(2,1)S(1)} collective-permute-done((bf16[160,1024]{1,0:T(8,128)(2,1)S(1)}, bf16[160,1024]{1,0:T(8,128)(2,1)S(1)}, u32[]{:S(2)}, u32[]{:S(2)}) %collective-permute-start.49) | collective-permute-done | bytes 327712 | tf_op jit(solution)/shard_map/ppermute | solution.py:15
  245.5 1.6 collective-permute-start.52
  250.4 4.6 %collective-permute-done.48 = bf16[160,1024]{1,0:T(8,128)(2,1)S(1)} collective-permute-done((bf16[160,1024]{1,0:T(8,128)(2,1)S(1)}, bf16[160,1024]{1,0:T(8,128)(2,1)S(1)}, u32[]{:S(2)}, u32[]{:S(2)}) %collective-permute-start.48) | collective-permute-done | bytes 327712 | tf_op jit(solution)/shard_map/ppermute | solution.py:15
  255.0 2.8 %collective-permute-done.47 = bf16[160,1024]{1,0:T(8,128)(2,1)S(1)} collective-permute-done((bf16[160,1024]{1,0:T(8,128)(2,1)S(1)}, bf16[160,1024]{1,0:T(8,128)(2,1)S(1)}, u32[]{:S(2)}, u32[]{:S(2)}) %collective-permute-start.47) | collective-permute-done | bytes 327712 | tf_op jit(solution)/shard_map/ppermute | solution.py:15
  257.9 3.4 %collective-permute-done.52 = bf16[320,1024]{1,0:T(8,128)(2,1)S(1)} collective-permute-done((bf16[320,1024]{1,0:T(8,128)(2,1)S(1)}, bf16[320,1024]{1,0:T(8,128)(2,1)S(1)}, u32[]{:S(2)}, u32[]{:S(2)}) %collective-permute-start.52) | collective-permute-done | bytes 655392 | tf_op jit(solution)/shard_map/ppermute | solution.py:20
  261.6 3.4 %collective-permute-done.45 = bf16[320,1024]{1,0:T(8,128)(2,1)S(1)} collective-permute-done((bf16[320,1024]{1,0:T(8,128)(2,1)S(1)}, bf16[320,1024]{1,0:T(8,128)(2,1)S(1)}, u32[]{:S(2)}, u32[]{:S(2)}) %collective-permute-start.45) | collective-permute-done | bytes 655392 | tf_op jit(solution)/shard_map/ppermute | solution.py:15
  266.3 4.5 %collective-permute-done.54 = bf16[320,1024]{1,0:T(8,128)(2,1)S(1)} collective-permute-done((bf16[320,1024]{1,0:T(8,128)(2,1)S(1)}, bf16[320,1024]{1,0:T(8,128)(2,1)S(1)}, u32[]{:S(2)}, u32[]{:S(2)}) %collective-permute-start.54) | collective-permute-done | bytes 655392 | tf_op jit(solution)/shard_map/ppermute | solution.py:15
  272.1 4.0 %collective-permute-done.53 = bf16[320,1024]{1,0:T(8,128)(2,1)S(1)} collective-permute-done((bf16[320,1024]{1,0:T(8,128)(2,1)S(1)}, bf16[320,1024]{1,0:T(8,128)(2,1)S(1)}, u32[]{:S(2)}, u32[]{:S(2)}) %collective-permute-start.53) | collective-permute-done | bytes 655392 | tf_op jit(solution)/shard_map/ppermute | solution.py:20
  276.1 1.8 collective-permute-done.55
  (159 shorter events, 67.3 us)
Async XLA Ops:
  3.4 6.5 %collective-permute-start = (bf16[176,256]{1,0:T(8,128)(2,1)}, bf16[176,256]{1,0:T(8,128)(2,1)}, u32[]{:S(2)}, u32[]{:S(2)}) collective-permute-start(bf16[176,256]{1,0:T(8,128)(2,1)} %get-tuple-element.147), channel_id=1, source_target_pairs={{0,1},{1,0},{2,3},{3,2},{4,5},{5,4},{6,7},{7,6},{8,9},{9,8},{10,11... | collective-permute-start | bytes 270344 | tf_op jit(solution)/shard_map/ppermute | solution.py:40
  3.8 6.3 %collective-permute-start.1 = (bf16[176,256]{1,0:T(8,128)(2,1)}, bf16[176,256]{1,0:T(8,128)(2,1)}, u32[]{:S(2)}, u32[]{:S(2)}) collective-permute-start(bf16[176,256]{1,0:T(8,128)(2,1)} %get-tuple-element.148), channel_id=1, source_target_pairs={{0,2},{1,3},{2,0},{3,1},{4,6},{5,7},{6,4},{7,5},{8,10},{9,11},{10,... | collective-permute-start | bytes 270344 | tf_op jit(solution)/shard_map/ppermute | solution.py:40
  8.0 18.5 %collective-permute-start.9 = (bf16[160,1024]{1,0:T(8,128)(2,1)S(1)}, bf16[160,1024]{1,0:T(8,128)(2,1)S(1)}, u32[]{:S(2)}, u32[]{:S(2)}) collective-permute-start(bf16[160,1024]{1,0:T(8,128)(2,1)S(1)} %get-tuple-element.127), channel_id=1, source_target_pairs={{0,3},{1,2},{2,1},{3,0},{4,7},{5,6},{6,5},{7,4},{8,11},{9,10},{10,... | collective-permute-start | bytes 983048 | tf_op jit(solution)/shard_map/ppermute | solution.py:40
  9.7 16.9 %collective-permute-start.4 = (bf16[160,1024]{1,0:T(8,128)(2,1)S(1)}, bf16[160,1024]{1,0:T(8,128)(2,1)S(1)}, u32[]{:S(2)}, u32[]{:S(2)}) collective-permute-start(bf16[160,1024]{1,0:T(8,128)(2,1)S(1)} %get-tuple-element.124), channel_id=1, source_target_pairs={{0,2},{1,3},{2,0},{3,1},{4,6},{5,7},{6,4},{7,5},{8,10},{9,11},{10,... | collective-permute-start | bytes 983048 | tf_op jit(solution)/shard_map/ppermute | solution.py:40
  32.0 9.8 %collective-permute-start.10 = (bf16[160,2048]{1,0:T(8,128)(2,1)S(1)}, bf16[160,2048]{1,0:T(8,128)(2,1)S(1)}, u32[]{:S(2)}, u32[]{:S(2)}) collective-permute-start(bf16[160,2048]{1,0:T(8,128)(2,1)S(1)} %convolution_convert_fusion.1), channel_id=1, source_target_pairs={{0,1},{1,0},{2,3},{3,2},{4,5},{5,4},{6,7},{7,6},{8,9},{9,8},{10,11... | collective-permute-start | bytes 1966088 | tf_op jit(solution)/shard_map/ppermute | solution.py:15
  33.7 10.6 %collective-permute-start.3 = (bf16[160,1024]{1,0:T(8,128)(2,1)S(1)}, bf16[160,1024]{1,0:T(8,128)(2,1)S(1)}, u32[]{:S(2)}, u32[]{:S(2)}) collective-permute-start(bf16[160,1024]{1,0:T(8,128)(2,1)S(1)} %get-tuple-element.125), channel_id=1, source_target_pairs={{0,1},{1,0},{2,3},{3,2},{4,5},{5,4},{6,7},{7,6},{8,9},{9,8},{10,11... | collective-permute-start | bytes 983048 | tf_op jit(solution)/shard_map/ppermute | solution.py:40
  42.7 16.4 %collective-permute-start.11 = (bf16[160,2048]{1,0:T(8,128)(2,1)S(1)}, bf16[160,2048]{1,0:T(8,128)(2,1)S(1)}, u32[]{:S(2)}, u32[]{:S(2)}) collective-permute-start(bf16[160,2048]{1,0:T(8,128)(2,1)S(1)} %fusion.28), channel_id=1, source_target_pairs={{0,2},{1,3},{2,0},{3,1},{4,6},{5,7},{6,4},{7,5},{8,10},{9,11},{10,... | collective-permute-start | bytes 1966088 | tf_op jit(solution)/shard_map/ppermute | solution.py:15
  62.5 18.7 %collective-permute-start.14 = (bf16[320,1024]{1,0:T(8,128)(2,1)S(1)}, bf16[320,1024]{1,0:T(8,128)(2,1)}, u32[]{:S(2)}, u32[]{:S(2)}) collective-permute-start(bf16[320,1024]{1,0:T(8,128)(2,1)S(1)} %get-tuple-element.71.refs_0_), channel_id=1, source_target_pairs={{0,8},{4,12},{8,16},{12,20},{16,24},{20,28},{24,0},{28,4},{1,9},{5... | collective-permute-start | bytes 1966088 | tf_op jit(solution)/shard_map/ppermute | solution.py:20
  63.6 17.6 %collective-permute-start.15 = (bf16[320,1024]{1,0:T(8,128)(2,1)S(1)}, bf16[320,1024]{1,0:T(8,128)(2,1)}, u32[]{:S(2)}, u32[]{:S(2)}) collective-permute-start(bf16[320,1024]{1,0:T(8,128)(2,1)S(1)} %get-tuple-element.71.refs_0_), channel_id=1, source_target_pairs={{0,4},{4,0},{8,12},{12,8},{16,20},{20,16},{24,28},{28,24},{1,5},{5... | collective-permute-start | bytes 1966088 | tf_op jit(solution)/shard_map/ppermute | solution.py:15
  65.1 16.3 %collective-permute-start.16 = (bf16[320,1024]{1,0:T(8,128)(2,1)S(1)}, bf16[320,1024]{1,0:T(8,128)(2,1)}, u32[]{:S(2)}, u32[]{:S(2)}) collective-permute-start(bf16[320,1024]{1,0:T(8,128)(2,1)S(1)} %get-tuple-element.71.refs_0_), channel_id=1, source_target_pairs={{0,2},{1,3},{2,0},{3,1},{4,6},{5,7},{6,4},{7,5},{8,10},{9,11},{10,... | collective-permute-start | bytes 1966088 | tf_op jit(solution)/shard_map/ppermute | solution.py:15
  81.4 22.1 %collective-permute-start.17 = (bf16[320,1024]{1,0:T(8,128)(2,1)}, bf16[320,1024]{1,0:T(8,128)(2,1)}, u32[]{:S(2)}, u32[]{:S(2)}) collective-permute-start(bf16[320,1024]{1,0:T(8,128)(2,1)} %collective-permute-done.14.refs_5_), channel_id=1, source_target_pairs={{0,8},{4,12},{8,16},{12,20},{16,24},{20,28},{24,0},{28,4},{1,9},{5... | collective-permute-start | bytes 1966088 | tf_op jit(solution)/shard_map/ppermute | solution.py:20
  83.0 23.4 %collective-permute-start.18 = (bf16[320,1024]{1,0:T(8,128)(2,1)}, bf16[320,1024]{1,0:T(8,128)(2,1)}, u32[]{:S(2)}, u32[]{:S(2)}) collective-permute-start(bf16[320,1024]{1,0:T(8,128)(2,1)} %collective-permute-done.14.refs_5_), channel_id=1, source_target_pairs={{0,4},{4,0},{8,12},{12,8},{16,20},{20,16},{24,28},{28,24},{1,5},{5... | collective-permute-start | bytes 1966088 | tf_op jit(solution)/shard_map/ppermute | solution.py:15
  83.5 24.4 %collective-permute-start.19 = (bf16[320,1024]{1,0:T(8,128)(2,1)}, bf16[320,1024]{1,0:T(8,128)(2,1)}, u32[]{:S(2)}, u32[]{:S(2)}) collective-permute-start(bf16[320,1024]{1,0:T(8,128)(2,1)} %collective-permute-done.14.refs_5_), channel_id=1, source_target_pairs={{0,2},{1,3},{2,0},{3,1},{4,6},{5,7},{6,4},{7,5},{8,10},{9,11},{10,... | collective-permute-start | bytes 1966088 | tf_op jit(solution)/shard_map/ppermute | solution.py:15
  85.0 16.4 %collective-permute-start.13 = (f32[4,2,16,160]{3,2,1,0:T(8,128)S(1)}, f32[4,2,16,160]{3,2,1,0:T(8,128)S(1)}, u32[]{:S(2)}, u32[]{:S(2)}) collective-permute-start(f32[4,2,16,160]{3,2,1,0:T(8,128)S(1)} %copy-done.9), channel_id=1, source_target_pairs={{0,2},{1,3},{2,0},{3,1},{4,6},{5,7},{6,4},{7,5},{8,10},{9,11},{10,... | collective-permute-start | bytes 245768 | tf_op jit(solution)/shard_map/ppermute | solution.py:15
  103.5 10.7 %collective-permute-start.21 = (bf16[160,1024]{1,0:T(8,128)(2,1)S(1)}, bf16[160,1024]{1,0:T(8,128)(2,1)S(1)}, u32[]{:S(2)}, u32[]{:S(2)}) collective-permute-start(bf16[160,1024]{1,0:T(8,128)(2,1)S(1)} %slice.166), channel_id=1, source_target_pairs={{0,2},{1,3},{2,0},{3,1},{4,6},{5,7},{6,4},{7,5},{8,10},{9,11},{10,... | collective-permute-start | bytes 983048 | tf_op jit(solution)/shard_map/ppermute | solution.py:15
  105.1 10.3 %collective-permute-start.22 = (bf16[160,1024]{1,0:T(8,128)(2,1)S(1)}, bf16[160,1024]{1,0:T(8,128)(2,1)S(1)}, u32[]{:S(2)}, u32[]{:S(2)}) collective-permute-start(bf16[160,1024]{1,0:T(8,128)(2,1)S(1)} %slice.167), channel_id=1, source_target_pairs={{0,4},{4,0},{8,12},{12,8},{16,20},{20,16},{24,28},{28,24},{1,5},{5... | collective-permute-start | bytes 983048 | tf_op jit(solution)/shard_map/ppermute | solution.py:15
  107.4 10.3 %collective-permute-start.23 = (bf16[160,1024]{1,0:T(8,128)(2,1)S(1)}, bf16[160,1024]{1,0:T(8,128)(2,1)S(1)}, u32[]{:S(2)}, u32[]{:S(2)}) collective-permute-start(bf16[160,1024]{1,0:T(8,128)(2,1)S(1)} %slice.168), channel_id=1, source_target_pairs={{0,2},{1,3},{2,0},{3,1},{4,6},{5,7},{6,4},{7,5},{8,10},{9,11},{10,... | collective-permute-start | bytes 983048 | tf_op jit(solution)/shard_map/ppermute | solution.py:15
  108.9 10.8 %collective-permute-start.24 = (bf16[160,1024]{1,0:T(8,128)(2,1)S(1)}, bf16[160,1024]{1,0:T(8,128)(2,1)S(1)}, u32[]{:S(2)}, u32[]{:S(2)}) collective-permute-start(bf16[160,1024]{1,0:T(8,128)(2,1)S(1)} %slice.169), channel_id=1, source_target_pairs={{0,4},{4,0},{8,12},{12,8},{16,20},{20,16},{24,28},{28,24},{1,5},{5... | collective-permute-start | bytes 983048 | tf_op jit(solution)/shard_map/ppermute | solution.py:15
  109.9 15.4 %collective-permute-start.20 = (bf16[320,1024]{1,0:T(8,128)(2,1)}, bf16[320,1024]{1,0:T(8,128)(2,1)S(1)}, u32[]{:S(2)}, u32[]{:S(2)}) collective-permute-start(bf16[320,1024]{1,0:T(8,128)(2,1)} %collective-permute-done.17.refs_0_), channel_id=1, source_target_pairs={{0,8},{4,12},{8,16},{12,20},{16,24},{20,28},{24,0},{28,4},{1,9},{5... | collective-permute-start | bytes 1966088 | tf_op jit(solution)/shard_map/ppermute | solution.py:20
  119.8 13.2 %collective-permute-start.25 = (bf16[320,1024]{1,0:T(8,128)(2,1)}, bf16[320,1024]{1,0:T(8,128)(2,1)S(1)}, u32[]{:S(2)}, u32[]{:S(2)}) collective-permute-start(bf16[320,1024]{1,0:T(8,128)(2,1)} %collective-permute-done.17.refs_0_), channel_id=1, source_target_pairs={{0,4},{4,0},{8,12},{12,8},{16,20},{20,16},{24,28},{28,24},{1,5},{5... | collective-permute-start | bytes 1966088 | tf_op jit(solution)/shard_map/ppermute | solution.py:15
  121.1 11.9 %collective-permute-start.26 = (bf16[320,1024]{1,0:T(8,128)(2,1)}, bf16[320,1024]{1,0:T(8,128)(2,1)S(1)}, u32[]{:S(2)}, u32[]{:S(2)}) collective-permute-start(bf16[320,1024]{1,0:T(8,128)(2,1)} %collective-permute-done.17.refs_0_), channel_id=1, source_target_pairs={{0,2},{1,3},{2,0},{3,1},{4,6},{5,7},{6,4},{7,5},{8,10},{9,11},{10,... | collective-permute-start | bytes 1966088 | tf_op jit(solution)/shard_map/ppermute | solution.py:15
  133.0 17.5 %collective-permute-start.27 = (bf16[320,1024]{1,0:T(8,128)(2,1)S(1)}, bf16[320,1024]{1,0:T(8,128)(2,1)S(1)}, u32[]{:S(2)}, u32[]{:S(2)}) collective-permute-start(bf16[320,1024]{1,0:T(8,128)(2,1)S(1)} %collective-permute-done.20.refs_5_), channel_id=1, source_target_pairs={{0,4},{4,0},{8,12},{12,8},{16,20},{20,16},{24,28},{28,24},{1,5},{5... | collective-permute-start | bytes 1966088 | tf_op jit(solution)/shard_map/ppermute | solution.py:15
  134.1 17.6 %collective-permute-start.28 = (bf16[320,1024]{1,0:T(8,128)(2,1)S(1)}, bf16[320,1024]{1,0:T(8,128)(2,1)S(1)}, u32[]{:S(2)}, u32[]{:S(2)}) collective-permute-start(bf16[320,1024]{1,0:T(8,128)(2,1)S(1)} %collective-permute-done.20.refs_5_), channel_id=1, source_target_pairs={{0,2},{1,3},{2,0},{3,1},{4,6},{5,7},{6,4},{7,5},{8,10},{9,11},{10,... | collective-permute-start | bytes 1966088 | tf_op jit(solution)/shard_map/ppermute | solution.py:15
  144.8 17.9 %collective-permute-start.32 = (bf16[512,2048]{1,0:T(8,128)(2,1)S(1)}, bf16[512,2048]{1,0:T(8,128)(2,1)S(1)}, u32[]{:S(2)}, u32[]{:S(2)}) collective-permute-start(bf16[512,2048]{1,0:T(8,128)(2,1)S(1)} %fusion.19), channel_id=1, source_target_pairs={{0,1},{1,0},{2,3},{3,2},{4,5},{5,4},{6,7},{7,6},{8,9},{9,8},{10,11... | collective-permute-start | bytes 6291464 | tf_op jit(solution)/shard_map/ppermute | solution.py:15
  145.2 17.5 %collective-permute-start.29 = (bf16[160,1024]{1,0:T(8,128)(2,1)S(1)}, bf16[160,1024]{1,0:T(8,128)(2,1)S(1)}, u32[]{:S(2)}, u32[]{:S(2)}) collective-permute-start(bf16[160,1024]{1,0:T(8,128)(2,1)S(1)} %slice.172), channel_id=1, source_target_pairs={{0,2},{1,3},{2,0},{3,1},{4,6},{5,7},{6,4},{7,5},{8,10},{9,11},{10,... | collective-permute-start | bytes 983048 | tf_op jit(solution)/shard_map/ppermute | solution.py:15
  146.5 16.2 %collective-permute-start.30 = (bf16[160,1024]{1,0:T(8,128)(2,1)S(1)}, bf16[160,1024]{1,0:T(8,128)(2,1)S(1)}, u32[]{:S(2)}, u32[]{:S(2)}) collective-permute-start(bf16[160,1024]{1,0:T(8,128)(2,1)S(1)} %slice.173), channel_id=1, source_target_pairs={{0,4},{4,0},{8,12},{12,8},{16,20},{20,16},{24,28},{28,24},{1,5},{5... | collective-permute-start | bytes 983048 | tf_op jit(solution)/shard_map/ppermute | solution.py:15
  151.7 16.2 %collective-permute-start.33 = (bf16[160,1024]{1,0:T(8,128)(2,1)S(1)}, bf16[160,1024]{1,0:T(8,128)(2,1)S(1)}, u32[]{:S(2)}, u32[]{:S(2)}) collective-permute-start(bf16[160,1024]{1,0:T(8,128)(2,1)S(1)} %slice.178), channel_id=1, source_target_pairs={{0,2},{1,3},{2,0},{3,1},{4,6},{5,7},{6,4},{7,5},{8,10},{9,11},{10,... | collective-permute-start | bytes 983048 | tf_op jit(solution)/shard_map/ppermute | solution.py:15
  152.9 15.0 %collective-permute-start.34 = (bf16[160,1024]{1,0:T(8,128)(2,1)S(1)}, bf16[160,1024]{1,0:T(8,128)(2,1)S(1)}, u32[]{:S(2)}, u32[]{:S(2)}) collective-permute-start(bf16[160,1024]{1,0:T(8,128)(2,1)S(1)} %slice.179), channel_id=1, source_target_pairs={{0,4},{4,0},{8,12},{12,8},{16,20},{20,16},{24,28},{28,24},{1,5},{5... | collective-permute-start | bytes 983048 | tf_op jit(solution)/shard_map/ppermute | solution.py:15
  172.2 17.1 %collective-permute-start.37 = (bf16[320,1024]{1,0:T(8,128)(2,1)S(1)}, bf16[320,1024]{1,0:T(8,128)(2,1)S(1)}, u32[]{:S(2)}, u32[]{:S(2)}) collective-permute-start(bf16[320,1024]{1,0:T(8,128)(2,1)S(1)} %get-tuple-element.91), channel_id=1, source_target_pairs={{0,4},{4,0},{8,12},{12,8},{16,20},{20,16},{24,28},{28,24},{1,5},{5... | collective-permute-start | bytes 1966088 | tf_op jit(solution)/shard_map/ppermute | solution.py:15
  173.2 17.0 %collective-permute-start.35 = (bf16[320,1024]{1,0:T(8,128)(2,1)S(1)}, bf16[320,1024]{1,0:T(8,128)(2,1)S(1)}, u32[]{:S(2)}, u32[]{:S(2)}) collective-permute-start(bf16[320,1024]{1,0:T(8,128)(2,1)S(1)} %get-tuple-element.88), channel_id=1, source_target_pairs={{0,2},{1,3},{2,0},{3,1},{4,6},{5,7},{6,4},{7,5},{8,10},{9,11},{10,... | collective-permute-start | bytes 1966088 | tf_op jit(solution)/shard_map/ppermute | solution.py:15
  184.2 16.1 %collective-permute-start.40 = (bf16[512,2048]{1,0:T(8,128)(2,1)S(1)}, bf16[512,2048]{1,0:T(8,128)(2,1)S(1)}, u32[]{:S(2)}, u32[]{:S(2)}) collective-permute-start(bf16[512,2048]{1,0:T(8,128)(2,1)S(1)} %fusion.22), channel_id=1, source_target_pairs={{0,1},{1,0},{2,3},{3,2},{4,5},{5,4},{6,7},{7,6},{8,9},{9,8},{10,11... | collective-permute-start | bytes 6291464 | tf_op jit(solution)/shard_map/ppermute | solution.py:15
  189.4 10.8 %collective-permute-start.39 = (bf16[160,1024]{1,0:T(8,128)(2,1)S(1)}, bf16[160,1024]{1,0:T(8,128)(2,1)S(1)}, u32[]{:S(2)}, u32[]{:S(2)}) collective-permute-start(bf16[160,1024]{1,0:T(8,128)(2,1)S(1)} %slice_add_fusion.14), channel_id=1, source_target_pairs={{0,2},{1,3},{2,0},{3,1},{4,6},{5,7},{6,4},{7,5},{8,10},{9,11},{10,... | collective-permute-start | bytes 983048 | tf_op jit(solution)/shard_map/ppermute | solution.py:15
  190.3 9.9 %collective-permute-start.38 = (bf16[160,1024]{1,0:T(8,128)(2,1)S(1)}, bf16[160,1024]{1,0:T(8,128)(2,1)S(1)}, u32[]{:S(2)}, u32[]{:S(2)}) collective-permute-start(bf16[160,1024]{1,0:T(8,128)(2,1)S(1)} %slice_add_fusion.15), channel_id=1, source_target_pairs={{0,4},{4,0},{8,12},{12,8},{16,20},{20,16},{24,28},{28,24},{1,5},{5... | collective-permute-start | bytes 983048 | tf_op jit(solution)/shard_map/ppermute | solution.py:15
  205.4 15.9 %collective-permute-start.42 = (bf16[320,1024]{1,0:T(8,128)(2,1)S(1)}, bf16[320,1024]{1,0:T(8,128)(2,1)S(1)}, u32[]{:S(2)}, u32[]{:S(2)}) collective-permute-start(bf16[320,1024]{1,0:T(8,128)(2,1)S(1)} %get-tuple-element.102), channel_id=1, source_target_pairs={{0,4},{4,0},{8,12},{12,8},{16,20},{20,16},{24,28},{28,24},{1,5},{5... | collective-permute-start | bytes 1966088 | tf_op jit(solution)/shard_map/ppermute | solution.py:15
  206.4 16.1 %collective-permute-start.41 = (bf16[320,1024]{1,0:T(8,128)(2,1)S(1)}, bf16[320,1024]{1,0:T(8,128)(2,1)S(1)}, u32[]{:S(2)}, u32[]{:S(2)}) collective-permute-start(bf16[320,1024]{1,0:T(8,128)(2,1)S(1)} %get-tuple-element.100), channel_id=1, source_target_pairs={{0,2},{1,3},{2,0},{3,1},{4,6},{5,7},{6,4},{7,5},{8,10},{9,11},{10,... | collective-permute-start | bytes 1966088 | tf_op jit(solution)/shard_map/ppermute | solution.py:15
  221.3 10.7 %collective-permute-start.50 = (bf16[160,1024]{1,0:T(8,128)(2,1)S(1)}, bf16[160,1024]{1,0:T(8,128)(2,1)S(1)}, u32[]{:S(2)}, u32[]{:S(2)}) collective-permute-start(bf16[160,1024]{1,0:T(8,128)(2,1)S(1)} %slice_add_fusion.4), channel_id=1, source_target_pairs={{0,2},{1,3},{2,0},{3,1},{4,6},{5,7},{6,4},{7,5},{8,10},{9,11},{10,... | collective-permute-start | bytes 983048 | tf_op jit(solution)/shard_map/ppermute | solution.py:15
  222.6 21.7 %collective-permute-start.44 = (bf16[320,1024]{1,0:T(8,128)(2,1)S(1)}, bf16[320,1024]{1,0:T(8,128)(2,1)S(1)}, u32[]{:S(2)}, u32[]{:S(2)}) collective-permute-start(bf16[320,1024]{1,0:T(8,128)(2,1)S(1)} %get-tuple-element.105), channel_id=1, source_target_pairs={{0,4},{4,0},{8,12},{12,8},{16,20},{20,16},{24,28},{28,24},{1,5},{5... | collective-permute-start | bytes 1966088 | tf_op jit(solution)/shard_map/ppermute | solution.py:15
  223.6 20.5 %collective-permute-start.49 = (bf16[160,1024]{1,0:T(8,128)(2,1)S(1)}, bf16[160,1024]{1,0:T(8,128)(2,1)S(1)}, u32[]{:S(2)}, u32[]{:S(2)}) collective-permute-start(bf16[160,1024]{1,0:T(8,128)(2,1)S(1)} %slice_add_fusion.6), channel_id=1, source_target_pairs={{0,4},{4,0},{8,12},{12,8},{16,20},{20,16},{24,28},{28,24},{1,5},{5... | collective-permute-start | bytes 983048 | tf_op jit(solution)/shard_map/ppermute | solution.py:15
  224.7 20.5 %collective-permute-start.51 = (bf16[320,1024]{1,0:T(8,128)(2,1)S(1)}, bf16[320,1024]{1,0:T(8,128)(2,1)S(1)}, u32[]{:S(2)}, u32[]{:S(2)}) collective-permute-start(bf16[320,1024]{1,0:T(8,128)(2,1)S(1)} %pad_maximum_fusion), channel_id=1, source_target_pairs={{0,8},{4,12},{8,16},{12,20},{16,24},{20,28},{24,0},{28,4},{1,9},{5... | collective-permute-start | bytes 1966088 | tf_op jit(solution)/shard_map/ppermute | solution.py:20
  226.4 20.7 %collective-permute-start.43 = (bf16[320,1024]{1,0:T(8,128)(2,1)S(1)}, bf16[320,1024]{1,0:T(8,128)(2,1)S(1)}, u32[]{:S(2)}, u32[]{:S(2)}) collective-permute-start(bf16[320,1024]{1,0:T(8,128)(2,1)S(1)} %get-tuple-element.103), channel_id=1, source_target_pairs={{0,2},{1,3},{2,0},{3,1},{4,6},{5,7},{6,4},{7,5},{8,10},{9,11},{10,... | collective-permute-start | bytes 1966088 | tf_op jit(solution)/shard_map/ppermute | solution.py:15
  244.3 10.7 %collective-permute-start.48 = (bf16[160,1024]{1,0:T(8,128)(2,1)S(1)}, bf16[160,1024]{1,0:T(8,128)(2,1)S(1)}, u32[]{:S(2)}, u32[]{:S(2)}) collective-permute-start(bf16[160,1024]{1,0:T(8,128)(2,1)S(1)} %slice_add_fusion.8), channel_id=1, source_target_pairs={{0,2},{1,3},{2,0},{3,1},{4,6},{5,7},{6,4},{7,5},{8,10},{9,11},{10,... | collective-permute-start | bytes 983048 | tf_op jit(solution)/shard_map/ppermute | solution.py:15
  245.5 15.8 %collective-permute-start.52 = (bf16[320,1024]{1,0:T(8,128)(2,1)S(1)}, bf16[320,1024]{1,0:T(8,128)(2,1)S(1)}, u32[]{:S(2)}, u32[]{:S(2)}) collective-permute-start(bf16[320,1024]{1,0:T(8,128)(2,1)S(1)} %maximum_add_fusion.1), channel_id=1, source_target_pairs={{0,8},{4,12},{8,16},{12,20},{16,24},{20,28},{24,0},{28,4},{1,9},{5... | collective-permute-start | bytes 1966088 | tf_op jit(solution)/shard_map/ppermute | solution.py:20
  247.1 10.7 %collective-permute-start.47 = (bf16[160,1024]{1,0:T(8,128)(2,1)S(1)}, bf16[160,1024]{1,0:T(8,128)(2,1)S(1)}, u32[]{:S(2)}, u32[]{:S(2)}) collective-permute-start(bf16[160,1024]{1,0:T(8,128)(2,1)S(1)} %slice_add_fusion.10), channel_id=1, source_target_pairs={{0,4},{4,0},{8,12},{12,8},{16,20},{20,16},{24,28},{28,24},{1,5},{5... | collective-permute-start | bytes 983048 | tf_op jit(solution)/shard_map/ppermute | solution.py:15
  248.0 17.1 %collective-permute-start.45 = (bf16[320,1024]{1,0:T(8,128)(2,1)S(1)}, bf16[320,1024]{1,0:T(8,128)(2,1)S(1)}, u32[]{:S(2)}, u32[]{:S(2)}) collective-permute-start(bf16[320,1024]{1,0:T(8,128)(2,1)S(1)} %get-tuple-element.106), channel_id=1, source_target_pairs={{0,2},{1,3},{2,0},{3,1},{4,6},{5,7},{6,4},{7,5},{8,10},{9,11},{10,... | collective-permute-start | bytes 1966088 | tf_op jit(solution)/shard_map/ppermute | solution.py:15
  248.9 21.8 %collective-permute-start.54 = (bf16[320,1024]{1,0:T(8,128)(2,1)S(1)}, bf16[320,1024]{1,0:T(8,128)(2,1)S(1)}, u32[]{:S(2)}, u32[]{:S(2)}) collective-permute-start(bf16[320,1024]{1,0:T(8,128)(2,1)S(1)} %get-tuple-element.118), channel_id=1, source_target_pairs={{0,4},{4,0},{8,12},{12,8},{16,20},{20,16},{24,28},{28,24},{1,5},{5... | collective-permute-start | bytes 1966088 | tf_op jit(solution)/shard_map/ppermute | solution.py:15
  261.5 14.6 %collective-permute-start.53 = (bf16[320,1024]{1,0:T(8,128)(2,1)S(1)}, bf16[320,1024]{1,0:T(8,128)(2,1)S(1)}, u32[]{:S(2)}, u32[]{:S(2)}) collective-permute-start(bf16[320,1024]{1,0:T(8,128)(2,1)S(1)} %maximum_add_fusion), channel_id=1, source_target_pairs={{0,8},{4,12},{8,16},{12,20},{16,24},{20,28},{24,0},{28,4},{1,9},{5... | collective-permute-start | bytes 1966088 | tf_op jit(solution)/shard_map/ppermute | solution.py:20
  265.1 11.0 %collective-permute-start.46 = (bf16[160,1024]{1,0:T(8,128)(2,1)S(1)}, bf16[160,1024]{1,0:T(8,128)(2,1)S(1)}, u32[]{:S(2)}, u32[]{:S(2)}) collective-permute-start(bf16[160,1024]{1,0:T(8,128)(2,1)S(1)} %slice_add_fusion.12), channel_id=1, source_target_pairs={{0,4},{4,0},{8,12},{12,8},{16,20},{20,16},{24,28},{28,24},{1,5},{5... | collective-permute-start | bytes 983048 | tf_op jit(solution)/shard_map/ppermute | solution.py:15
  270.8 7.1 %collective-permute-start.55 = (bf16[160,1024]{1,0:T(8,128)(2,1)S(1)}, bf16[160,1024]{1,0:T(8,128)(2,1)S(1)}, u32[]{:S(2)}, u32[]{:S(2)}) collective-permute-start(bf16[160,1024]{1,0:T(8,128)(2,1)S(1)} %slice_add_fusion.1), channel_id=1, source_target_pairs={{0,2},{1,3},{2,0},{3,1},{4,6},{5,7},{6,4},{7,5},{8,10},{9,11},{10,... | collective-permute-start | bytes 983048 | tf_op jit(solution)/shard_map/ppermute | solution.py:15
  (22 other events, 338.7 us)
where the time goes:
time: 284 us; the launch traced here: 279 us
  waiting for transfers between devices  133 us (47%)
  starting transfers between devices  56.4 us (20%)
  Pallas kernels  36.7 us (13%)
  matrix products  36.2 us (13%)
  local copies, waits for them, and re-layouts  10.3 us (4%)
  other arithmetic  4.06 us (1%)
    ppermute x41, waiting for transfers between devices, partner_2(): return lax.ppermute(value, axis, pairs)  102 us
    ppermute x41, starting transfers between devices, partner_2(): return lax.ppermute(value, axis, pairs)  39 us
    ppermute x6, waiting for transfers between devices, shift_z(): lax.ppermute(value, 'grp', [(g, (g + 2) % groups) for g in range(groups)])  24.9 us
    dot_general x4, matrix products, run_expert(): jnp.dot(rows, up_gate_weight[0], preferred_element_type=jnp.float32)  22.4 us
    pallas_call x4, Pallas kernels, attend_block(): pl.pallas_call(functools.partial(attend_kernel, index), out_shape=jax.Sha...  18.4 us
    dot_general x4, matrix products, run_expert(): jnp.dot(hidden, down_weight[0], preferred_element_type=jnp.float32)  10 us
    pallas_call x2, Pallas kernels, pick_rows(): pl.pallas_call(functools.partial(pick_kernel, capacity), out_shape=(shape...  9.4 us
    pallas_call x2, Pallas kernels, combine_rows(): pl.pallas_call(combine_kernel, out_shape=[kept, kept, sent] * (blocks //...  7.57 us
  transfers between devices with their start and end apart: 56, of which 32 were waited for; matrix products, arithmetic and copies ran while one was open for 15% of the time, Pallas kernels for 8%

commit v1 on v0

--- a/solution.py
+++ b/solution.py
@@ -214,30 +214,36 @@
             axis=0,
         )
         weight = weight.T.astype(jnp.bfloat16)
-        level, (far_x, far_y) = block // 4, (block // 2 % 2, block % 2)
+        far_x, far_y = block // 2, block % 2
         for side in range(2):
             inner = pl.ds(block * capacity, capacity), pl.ds(side * half, half)
             both = jnp.concatenate([own_ref[inner], other_ref[inner]], axis=0)
             share = jnp.dot(weight, both, preferred_element_type=jnp.float32).astype(jnp.bfloat16)
             sent, place = (far_x, far_y) if side else (far_y, far_x)
             if sent:
-                out_refs[6 * level + 3 * side + 2][pl.ds(place * rows, rows), :] = share
+                out_refs[3 * side + 2][pl.ds(place * rows, rows), :] = share
             else:
-                out_refs[6 * level + 3 * side + place][...] = share
-
-
-def combine_rows(place, gate, own, other):
+                out_refs[3 * side + place][...] = share
+
+
+def combine_rows(part, parts, place, gate, own, other):
     blocks, _, rows = place.shape
     half = own.shape[1] // 2
     kept = jax.ShapeDtypeStruct((rows, half), jnp.bfloat16)
     sent = jax.ShapeDtypeStruct((2 * rows, half), jnp.bfloat16)
+    count = own.shape[0] // parts
+    whole = lambda shape: pl.BlockSpec(shape, lambda j: (0,) * len(shape))
+    level = pl.BlockSpec((count, 2 * half), lambda j: (part, 0))
     return pl.pallas_call(
         combine_kernel,
-        out_shape=[kept, kept, sent] * (blocks // 2),
-        compiler_params=pltpu.CompilerParams(vmem_limit_bytes=48 * 2**20),
+        out_shape=[kept, kept, sent] * 2,
+        grid=(1,),
+        in_specs=[whole(place.shape), whole(gate.shape), level, level],
+        out_specs=[whole(kept.shape), whole(kept.shape), whole(sent.shape)] * 2,
+        compiler_params=pltpu.CompilerParams(vmem_limit_bytes=44 * 2**20),
         cost_estimate=pl.CostEstimate(
-            flops=8 * own.shape[0] * rows * half,
-            bytes_accessed=4 * (blocks * rows + 2 * own.shape[0]) * half,
+            flops=8 * count * rows * half,
+            bytes_accessed=4 * (blocks * rows + 2 * count) * half,
             transcendentals=0,
         ),
     )(place, gate, own, other)
@@ -276,37 +282,81 @@
     return jnp.where(wanted, place, -1), gate
 
 
+def expert_kernel(rows_ref, gate_ref, up_ref, down_ref, out_ref, total):
+    step = pl.program_id(0)
+    rows = rows_ref[...]
+    gate = jnp.dot(rows, gate_ref[0], preferred_element_type=jnp.float32)
+    up = jnp.dot(rows, up_ref[0], preferred_element_type=jnp.float32)
+    hidden = (gate / (1.0 + jnp.exp(-gate)) * up).astype(jnp.bfloat16)
+    part = jnp.dot(hidden, down_ref[0], preferred_element_type=jnp.float32)
+    last = pl.num_programs(0) - 1
+
+    @pl.when(step == 0)
+    def _():
+        total[...] = part
+
+    @pl.when((step > 0) & (step < last))
+    def _():
+        total[...] += part
+
+    @pl.when(step == last)
+    def _():
+        out_ref[...] = (total[...] + part).astype(jnp.bfloat16)
+
+
 def run_expert(rows, up_gate_weight, down_weight):
+    count, width = rows.shape
     hidden_width = down_weight.shape[1]
-    projected = jnp.dot(rows, up_gate_weight[0], preferred_element_type=jnp.float32)
-    hidden = (jax.nn.silu(projected[:, :hidden_width]) * projected[:, hidden_width:]).astype(
-        jnp.bfloat16
-    )
-    return jnp.dot(hidden, down_weight[0], preferred_element_type=jnp.float32).astype(jnp.bfloat16)
-
-
-def experts_by_gather(packed, place, gate, capacity, up_gate_weight, down_weight):
+    tile = 256
+    steps = hidden_width // tile
+    return pl.pallas_call(
+        expert_kernel,
+        out_shape=jax.ShapeDtypeStruct((count, width), jnp.bfloat16),
+        grid=(steps,),
+        in_specs=[
+            pl.BlockSpec((count, width), lambda j: (0, 0)),
+            pl.BlockSpec((1, width, tile), lambda j: (0, 0, j)),
+            pl.BlockSpec((1, width, tile), lambda j: (0, 0, j + steps)),
+            pl.BlockSpec((1, tile, width), lambda j: (0, j, 0)),
+        ],
+        out_specs=pl.BlockSpec((count, width), lambda j: (0, 0)),
+        scratch_shapes=[pltpu.VMEM((count, width), jnp.float32)],
+        compiler_params=pltpu.CompilerParams(vmem_limit_bytes=44 * 2**20),
+        cost_estimate=pl.CostEstimate(
+            flops=6 * count * width * hidden_width,
+            bytes_accessed=6 * width * hidden_width + 4 * count * width,
+            transcendentals=count * hidden_width,
+        ),
+    )(rows, up_gate_weight, up_gate_weight, down_weight)
+
+
+def experts_by_gather(packed, routing, top_count, capacity, up_gate_weight, down_weight):
     depth = lax.axis_size("grp") // 2
-    per_level = place.shape[0] // depth
     rows = packed.shape[0] // 2
+    routing = routing_pair(after(routing, packed), swap_x)
     lines, beside_x, beside_y, diagonal = [packed], [], [], []
+    halves = []
 
     def cross(level, earlier):
-        first_x, second_y = beside_x[level][:rows], beside_y[level][rows:]
+        first_x, second_y = halves[level]
         if earlier is not None:
-            first_x, second_y = after(first_x, earlier), after(second_y, earlier)
+            first_x, second_y = after(first_x, *earlier), after(second_y, *earlier)
         diagonal.append((swap_y(first_x), swap_x(second_y)))
 
     for level in range(depth):
         line = lines[level]
+        if level == 1:
+            line = after(line, routing)
+            routing = routing_pair(after(routing, *halves[0]), swap_y)
         if level == 2:
-            cross(0, line)
-            cross(1, line)
+            cross(0, (line, routing))
+            cross(1, (line,))
             line = after(line, *diagonal[0], *diagonal[1])
         elif level > 2:
             line = after(line, beside_x[level - 1], beside_y[level - 1])
         beside_x.append(swap_x(line))
         beside_y.append(swap_y(line))
+        halves.append((beside_x[level][:rows], beside_y[level][rows:]))
         if level + 1 < depth:
             line = lines[level]
             if level:
@@ -314,7 +364,21 @@
             lines.append(shift_z(line))
     for level in range(len(diagonal), depth):
         cross(level, None)
-    kept, sent, back, joined = {}, {}, {}, {}
+    if depth == 1:
+        routing = routing_pair(routing, swap_y)
+    place, gate = selections(routing, top_count)
+    per_level = place.shape[0] // depth
+    results, kept, sent, back, joined = {}, {}, {}, {}, {}
+
+    def combine(level, *earlier):
+        index, count, own_result, other_result = results[level]
+        if earlier:
+            own_result = after(own_result, *earlier)
+        blocks = slice(level * per_level, (level + 1) * per_level)
+        parts = combine_rows(index, count, place[blocks], gate[blocks], own_result, other_result)
+        first, first_x, first_sent, second, second_y, second_sent = parts
+        kept[level] = first, first_x, second, second_y
+        sent[level] = first_sent, second_sent
 
     def send_back(level, *earlier):
         first_sent, second_sent = sent[level]
@@ -335,18 +399,17 @@
         for level in levels:
             gathered += [lines[level], beside_y[level], beside_x[level], *diagonal[level]]
         ahead, last = levels[-1] + 1, levels[-1] + 2
-        if last < depth:
-            gathered[0] = after(gathered[0], lines[last])
         if start:
             gathered[0] = after(gathered[0], kept[start - 1][0])
         blocks = slice(start * per_level, (start + len(levels)) * per_level)
         own, sibling = pick_rows(capacity, place[blocks], gathered)
         if last < depth:
-            sibling = after(sibling, beside_x[ahead], beside_y[ahead])
+            sibling = after(sibling, beside_x[ahead], beside_y[ahead], lines[last])
         other = swap_core(sibling)
         other_result = run_expert(other, up_gate_weight, down_weight)
         if last < depth:
-            own = after(own, beside_x[last], beside_y[last])
+            other_result = after(other_result, beside_x[last], beside_y[last])
+            own = after(own, other_result)
         if start:
             back[start - 1] = tuple(after(part, other_result) for part in back[start - 1])
             join(start - 1)
@@ -357,20 +420,15 @@
             own_result = after(own_result, *diagonal[ahead])
         if start:
             own_result = after(own_result, *joined[start - 1])
-        parts = combine_rows(place[blocks], gate[blocks], own_result, other_result)
         for index, level in enumerate(levels):
-            first, first_x, first_sent, second, second_y, second_sent = parts[
-                6 * index : 6 * index + 6
-            ]
-            kept[level] = first, first_x, second, second_y
-            sent[level] = first_sent, second_sent
-        levels = [level for level in levels if level]
+            results[level] = index, len(levels), own_result, other_result
+            if level:
+                combine(level)
+                send_back(level, *back.get(level - 1, ()))
         for level in levels:
-            send_back(level, *back.get(level - 1, ()))
-        if ahead < depth:
-            levels = levels[:-1]
-        for level in levels:
-            join(level)
+            if level and (ahead >= depth or level < levels[-1]):
+                join(level)
+    combine(0, *(kept[depth - 1][:1] if depth > 1 else ()))
     send_back(0, *back.get(depth - 1, ()))
     join(0)
     shares = {}
@@ -436,16 +494,15 @@
     own = share_of(0, query_blocks[0])
     routing = routing_start(own_live, expert_ids, gate_values, own)
     far_core = share_of(3, after(query_blocks[3], query_blocks[2], own, routing))
-    routing = routing_pair(routing, swap_x)
-    far = share_of(2, after(query_blocks[2], routing)) + swap_core(far_core)
+    far = share_of(2, query_blocks[2]) + swap_core(far_core)
     near = share_of(1, after(query_blocks[1], far))
     far = swap_y(far)
     attended, packed = normalize(
         lengths[0], own, swap_core(after(near, far)), far, residual, norm_gain[None, :]
     )
-    routing = routing_pair(after(routing, packed), swap_y)
-    place, gate = selections(routing, top_count)
-    moe_out = experts_by_gather(packed, place, gate, capacity, up_gate_weight, down_weight)
+    moe_out = experts_by_gather(
+        packed, routing, top_count, capacity, up_gate_weight, down_weight
+    )
     return (attended, moe_out)
 
 

time: 284 us -> 269 us (0.947)
  matrix products: 36.2 us -> 3.76 us
  Pallas kernels: 36.7 us -> 61.9 us
  local copies, waits for them, and re-layouts: 10.3 us -> 5.43 us
  waiting for transfers between devices: 133 us -> 129 us
  starting transfers between devices: 56.4 us -> 59.7 us
    dot_general x8 -> x0, matrix products: 32.4 us -> none  [the longest x4 22.4 us: run_expert(): jnp.dot(rows, up_gate_weight[0], preferred_element_type=jnp.float32)]
    pallas_call x2 -> x8, Pallas kernels: 7.57 us -> 38.5 us  [the longest x4 34 us: run_expert(): pl.pallas_call(expert_kernel, out_shape=jax.ShapeDtypeStruct((count, widt...]
    ppermute x6, waiting for transfers between devices: 24.9 us -> 7.53 us  [shift_z(): lax.ppermute(value, 'grp', [(g, (g + 2) % groups) for g in range(groups)])]
    ppermute x41, waiting for transfers between devices: 102 us -> 114 us  [partner_2(): return lax.ppermute(value, axis, pairs)]
    slice x10 -> x11, local copies, waits for them, and re-layouts: 4.08 us -> 0.19 us  [the longest x8 0.18 us: experts_by_gather(): halves.append((beside_x[level][:rows], beside_y[level][rows:]))]
    pallas_call x4, Pallas kernels: 18.4 us -> 14.5 us  [attend_block(): pl.pallas_call(functools.partial(attend_kernel, index), out_shape=jax.Sha...]
  transfers between devices with their start and end apart: 56 -> 56, of which waited for: 32 -> 32; matrix products, arithmetic and copies ran while one was open for 15% -> 2% of each run, Pallas kernels for 8% -> 20%
where the time goes in v1:
time: 269 us; the launch traced here: 265 us
  waiting for transfers between devices  129 us (48%)
  Pallas kernels  61.9 us (23%)
  starting transfers between devices  59.7 us (22%)
  local copies, waits for them, and re-layouts  5.43 us (2%)
  matrix products  3.76 us (1%)
  other arithmetic  2.83 us (1%)
    ppermute x41, waiting for transfers between devices, partner_2(): return lax.ppermute(value, axis, pairs)  114 us
    ppermute x41, starting transfers between devices, partner_2(): return lax.ppermute(value, axis, pairs)  41.3 us
    pallas_call x4, Pallas kernels, run_expert(): pl.pallas_call(expert_kernel, out_shape=jax.ShapeDtypeStruct((count, widt...  34 us
    pallas_call x4, Pallas kernels, attend_block(): pl.pallas_call(functools.partial(attend_kernel, index), out_shape=jax.Sha...  14.5 us
    ppermute x6, starting transfers between devices, shift_z(): lax.ppermute(value, 'grp', [(g, (g + 2) % groups) for g in range(groups)])  7.77 us
    pallas_call x2, Pallas kernels, pick_rows(): pl.pallas_call(functools.partial(pick_kernel, capacity), out_shape=(shape...  7.57 us
    ppermute x6, waiting for transfers between devices, shift_z(): lax.ppermute(value, 'grp', [(g, (g + 2) % groups) for g in range(groups)])  7.53 us
    ppermute x6, starting transfers between devices, xor_group(): lax.ppermute(value, 'sp', [(s, s ^ mask) for s in range(lax.axis_size('sp...  5.75 us
  transfers between devices with their start and end apart: 56, of which 32 were waited for; matrix products, arithmetic and copies ran while one was open for 2% of the time, Pallas kernels for 20%

profile of v1, /device:TPU:0, one launch (start us, length us, event | category | flops | bytes accessed | tf_op | source)
XLA Modules:
  0.0 265.1 jit_solution(6146797679785677880)
XLA Ops:
  2.6 2.5 collective-permute-start.2
  5.8 2.1 collective-permute-start.4
  8.0 3.2 %collective-permute-done.1.refs_2_ = bf16[176,256]{1,0:T(8,128)(2,1)S(1)} collective-permute-done((bf16[176,256]{1,0:T(8,128)(2,1)S(1)}, bf16[176,256]{1,0:T(8,128)(2,1)S(1)}, u32[]{:S(2)}, u32[]{:S(2)}) %collective-permute-start.1) | collective-permute-done | bytes 90144 | tf_op jit(solution)/shard_map/ppermute | solution.py:40
  11.2 3.6 %shard_map.122 = bf16[160,1024]{1,0:T(8,128)(2,1)S(1)} custom-call(s32[1]{0:T(128)} %bitcast.1.mine_ref, bf16[160,1024]{1,0:T(8,128)(2,1)S(1)} %get-tuple-element.130.query_ref, bf16[512,256]{1,0:T(8,128)(2,1)S(1)} %bitcast.40, bf16[176,256]{1,0:T(8,128)(2,1)S(1)} %get-tuple-element.157.refs_0_, bf16[176,256]{1,0:T(8,128)(2,1)S(1)} %collective-permute-done.refs_1_, ...), custom_call_target="tpu_custom_call" | custom-call | flops 754974720 | bytes 1245184 | tf_op jit(solution)/shard_map/pallas_call | solution.py:100
  15.7 3.7 %collective-permute-start.8 = (f32[16,160]{1,0:T(8,128)S(1)}, f32[16,160]{1,0:T(8,128)S(1)}, u32[]{:S(2)}, u32[]{:S(2)}) collective-permute-start(f32[16,160]{1,0:T(8,128)S(1)} %maximum_bitcast_fusion), channel_id=1, source_target_pairs={{0,24},{4,28},{8,0},{12,4},{16,8},{20,12},{24,16},{28,20},{1,25},{... | collective-permute-start | bytes 30728 | tf_op jit(solution)/shard_map/ppermute | solution.py:259
  20.9 3.2 %collective-permute-done.7 = f32[16,160]{1,0:T(8,128)S(1)} collective-permute-done((f32[16,160]{1,0:T(8,128)S(1)}, f32[16,160]{1,0:T(8,128)S(1)}, u32[]{:S(2)}, u32[]{:S(2)}) %collective-permute-start.7) | collective-permute-done | bytes 10272 | tf_op jit(solution)/shard_map/ppermute | solution.py:259
  25.1 3.6 %shard_map.124 = bf16[160,1024]{1,0:T(8,128)(2,1)S(1)} custom-call(s32[1]{0:T(128)} %bitcast.1.mine_ref, bf16[160,1024]{1,0:T(8,128)(2,1)S(1)} %collective-permute-done.5.query_ref, bf16[512,256]{1,0:T(8,128)(2,1)S(1)} %bitcast.41, bf16[176,256]{1,0:T(8,128)(2,1)S(1)} %get-tuple-element.157.refs_0_, bf16[176,256]{1,0:T(8,128)(2,1)S(1)} %collective-permute-done.refs_1_, ...), custom_call_target="tpu_custom_call" | custom-call | flops 754974720 | bytes 1245184 | tf_op jit(solution)/shard_map/pallas_call | solution.py:100
  30.2 3.6 %shard_map.123 = bf16[160,1024]{1,0:T(8,128)(2,1)S(1)} custom-call(s32[1]{0:T(128)} %bitcast.1.mine_ref, bf16[160,1024]{1,0:T(8,128)(2,1)S(1)} %collective-permute-done.4.query_ref, bf16[512,256]{1,0:T(8,128)(2,1)S(1)} %bitcast.42, bf16[176,256]{1,0:T(8,128)(2,1)S(1)} %get-tuple-element.157.refs_0_, bf16[176,256]{1,0:T(8,128)(2,1)S(1)} %collective-permute-done.refs_1_, ...), custom_call_target="tpu_custom_call" | custom-call | flops 754974720 | bytes 1245184 | tf_op jit(solution)/shard_map/pallas_call | solution.py:100
  36.1 3.6 %shard_map.125 = bf16[160,1024]{1,0:T(8,128)(2,1)S(1)} custom-call(s32[1]{0:T(128)} %bitcast.1.mine_ref, bf16[160,1024]{1,0:T(8,128)(2,1)S(1)} %collective-permute-done.3.query_ref, bf16[512,256]{1,0:T(8,128)(2,1)S(1)} %bitcast.43, bf16[176,256]{1,0:T(8,128)(2,1)S(1)} %get-tuple-element.157.refs_0_, bf16[176,256]{1,0:T(8,128)(2,1)S(1)} %collective-permute-done.refs_1_, ...), custom_call_target="tpu_custom_call" | custom-call | flops 754974720 | bytes 1245184 | tf_op jit(solution)/shard_map/pallas_call | solution.py:100
  40.8 10.7 %collective-permute-done.10.far_ref = bf16[160,2048]{1,0:T(8,128)(2,1)S(1)} collective-permute-done((bf16[160,2048]{1,0:T(8,128)(2,1)S(1)}, bf16[160,2048]{1,0:T(8,128)(2,1)S(1)}, u32[]{:S(2)}, u32[]{:S(2)}) %collective-permute-start.10) | collective-permute-done | bytes 655392 | tf_op jit(solution)/shard_map/ppermute | solution.py:15
  51.5 2.1 collective-permute-done.11.core_ref
  56.1 1.7 collective-permute-start.14
  60.7 14.8 %collective-permute-done.12 = f32[4,16,160]{2,1,0:T(8,128)S(1)} collective-permute-done((f32[4,16,160]{2,1,0:T(8,128)S(1)}, f32[4,16,160]{2,1,0:T(8,128)S(1)}, u32[]{:S(2)}, u32[]{:S(2)}) %collective-permute-start.12) | collective-permute-done | bytes 40992 | tf_op jit(solution)/shard_map/ppermute | solution.py:15
  75.9 1.6 collective-permute-start.17
  79.0 1.8 collective-permute-start.15
  80.9 12.8 %collective-permute-done.15 = f32[4,2,16,160]{3,2,1,0:T(8,128)S(1)} collective-permute-done((f32[4,2,16,160]{3,2,1,0:T(8,128)S(1)}, f32[4,2,16,160]{3,2,1,0:T(8,128)S(1)}, u32[]{:S(2)}, u32[]{:S(2)}) %collective-permute-start.15) | collective-permute-done | bytes 81952 | tf_op jit(solution)/shard_map/ppermute | solution.py:15
  98.1 1.6 collective-permute-start.26
  99.8 4.8 %collective-permute-done.18.refs_3_ = bf16[160,1024]{1,0:T(8,128)(2,1)S(1)} collective-permute-done((bf16[160,1024]{1,0:T(8,128)(2,1)S(1)}, bf16[160,1024]{1,0:T(8,128)(2,1)S(1)}, u32[]{:S(2)}, u32[]{:S(2)}) %collective-permute-start.18) | collective-permute-done | bytes 327712 | tf_op jit(solution)/shard_map/ppermute | solution.py:15
  104.9 3.5 %collective-permute-done.22.refs_8_ = bf16[160,1024]{1,0:T(8,128)(2,1)S(1)} collective-permute-done((bf16[160,1024]{1,0:T(8,128)(2,1)S(1)}, bf16[160,1024]{1,0:T(8,128)(2,1)S(1)}, u32[]{:S(2)}, u32[]{:S(2)}) %collective-permute-start.22) | collective-permute-done | bytes 327712 | tf_op jit(solution)/shard_map/ppermute | solution.py:15
  108.5 1.7 collective-permute-start.25
  115.2 3.2 %shard_map.127 = (bf16[512,2048]{1,0:T(8,128)(2,1)}, bf16[512,2048]{1,0:T(8,128)(2,1)}) custom-call(s32[8,2,160]{2,1,0:T(2,128)S(1)} %get-tuple-element.153.place_ref, bf16[320,1024]{1,0:T(8,128)(2,1)S(1)} %copy-done.8, bf16[320,1024]{1,0:T(8,128)(2,1)S(1)} %collective-permute-done.14.refs_1_, bf16[320,1024]{1,0:T(8,128)(2,1)S(1)} %collective-permute-done.13.refs_2_, ...), custom_call_target="tpu_custom_call" | custom-call | flops 671088640 | bytes 9437184 | tf_op jit(solution)/shard_map/pallas_call | solution.py:187
  118.5 4.0 %collective-permute-done.25.refs_1_ = bf16[320,1024]{1,0:T(8,128)(2,1)S(1)} collective-permute-done((bf16[320,1024]{1,0:T(8,128)(2,1)}, bf16[320,1024]{1,0:T(8,128)(2,1)S(1)}, u32[]{:S(2)}, u32[]{:S(2)}) %collective-permute-start.25) | collective-permute-done | bytes 655392 | tf_op jit(solution)/shard_map/ppermute | solution.py:15
  125.7 2.0 collective-permute-done.27.rows_ref
  127.7 8.1 %shard_map.128 = bf16[512,2048]{1,0:T(8,128)(2,1)S(1)} custom-call(bf16[512,2048]{1,0:T(8,128)(2,1)S(1)} %collective-permute-done.27.rows_ref, bf16[1,2048,1536]{2,1,0:T(8,128)(2,1)} %up_ref.7, bf16[1,2048,1536]{2,1,0:T(8,128)(2,1)} %up_ref.7, bf16[1,768,2048]{2,1,0:T(8,128)(2,1)S(1)} %copy-done), custom_call_target="tpu_custom_call" | custom-call | flops 4831838208 | bytes 13631488 | tf_op jit(solution)/shard_map/pallas_call | solution.py:312
  135.8 4.7 %collective-permute-done.29.refs_6_ = bf16[320,1024]{1,0:T(8,128)(2,1)S(1)} collective-permute-done((bf16[320,1024]{1,0:T(8,128)(2,1)S(1)}, bf16[320,1024]{1,0:T(8,128)(2,1)S(1)}, u32[]{:S(2)}, u32[]{:S(2)}) %collective-permute-start.29) | collective-permute-done | bytes 655392 | tf_op jit(solution)/shard_map/ppermute | solution.py:15
  141.3 1.6 collective-permute-start.31
  145.7 8.1 %shard_map.129.own_ref = bf16[512,2048]{1,0:T(8,128)(2,1)S(1)} custom-call(bf16[512,2048]{1,0:T(8,128)(2,1)S(1)} %copy-done.1, bf16[1,2048,1536]{2,1,0:T(8,128)(2,1)} %up_ref.7, bf16[1,2048,1536]{2,1,0:T(8,128)(2,1)} %up_ref.7, bf16[1,768,2048]{2,1,0:T(8,128)(2,1)S(1)} %copy-done), custom_call_target="tpu_custom_call" | custom-call | flops 4831838208 | bytes 13631488 | tf_op jit(solution)/shard_map/pallas_call | solution.py:312
  153.8 1.9 shard_map.130
  155.7 2.8 %collective-permute-done.34.refs_9_ = bf16[160,1024]{1,0:T(8,128)(2,1)S(1)} collective-permute-done((bf16[160,1024]{1,0:T(8,128)(2,1)S(1)}, bf16[160,1024]{1,0:T(8,128)(2,1)S(1)}, u32[]{:S(2)}, u32[]{:S(2)}) %collective-permute-start.34) | collective-permute-done | bytes 327712 | tf_op jit(solution)/shard_map/ppermute | solution.py:15
  159.8 4.3 %shard_map.131 = (bf16[512,2048]{1,0:T(8,128)(2,1)}, bf16[512,2048]{1,0:T(8,128)(2,1)}) custom-call(s32[8,2,160]{2,1,0:T(2,128)S(1)} %get-tuple-element.152.place_ref, bf16[320,1024]{1,0:T(8,128)(2,1)} %collective-permute-done.17.refs_0_, bf16[320,1024]{1,0:T(8,128)(2,1)S(1)} %collective-permute-done.25.refs_1_, ...), custom_call_target="tpu_custom_call" | custom-call | flops 671088640 | bytes 9437184 | tf_op jit(solution)/shard_map/pallas_call | solution.py:187
  165.9 2.6 collective-permute-done.36.rows_ref
  168.5 9.6 %shard_map.132 = bf16[512,2048]{1,0:T(8,128)(2,1)} custom-call(bf16[512,2048]{1,0:T(8,128)(2,1)S(1)} %collective-permute-done.36.rows_ref, bf16[1,2048,1536]{2,1,0:T(8,128)(2,1)} %up_ref.7, bf16[1,2048,1536]{2,1,0:T(8,128)(2,1)} %up_ref.7, bf16[1,768,2048]{2,1,0:T(8,128)(2,1)S(1)} %copy-done), custom_call_target="tpu_custom_call" | custom-call | flops 4831838208 | bytes 13631488 | tf_op jit(solution)/shard_map/pallas_call | solution.py:312
  178.2 4.2 %collective-permute-done.37 = bf16[320,1024]{1,0:T(8,128)(2,1)S(1)} collective-permute-done((bf16[320,1024]{1,0:T(8,128)(2,1)}, bf16[320,1024]{1,0:T(8,128)(2,1)S(1)}, u32[]{:S(2)}, u32[]{:S(2)}) %collective-permute-start.37) | collective-permute-done | bytes 655392 | tf_op jit(solution)/shard_map/ppermute | solution.py:15
  184.0 8.3 %shard_map.133.own_ref = bf16[512,2048]{1,0:T(8,128)(2,1)S(1)} custom-call(bf16[512,2048]{1,0:T(8,128)(2,1)S(1)} %copy-done.2, bf16[1,2048,1536]{2,1,0:T(8,128)(2,1)} %up_ref.7, bf16[1,2048,1536]{2,1,0:T(8,128)(2,1)} %up_ref.7, bf16[1,768,2048]{2,1,0:T(8,128)(2,1)S(1)} %copy-done), custom_call_target="tpu_custom_call" | custom-call | flops 4831838208 | bytes 13631488 | tf_op jit(solution)/shard_map/pallas_call | solution.py:312
  193.3 1.6 collective-permute-start.42
  197.0 11.8 %collective-permute-done.42 = bf16[320,1024]{1,0:T(8,128)(2,1)S(1)} collective-permute-done((bf16[320,1024]{1,0:T(8,128)(2,1)S(1)}, bf16[320,1024]{1,0:T(8,128)(2,1)S(1)}, u32[]{:S(2)}, u32[]{:S(2)}) %collective-permute-start.42) | collective-permute-done | bytes 655392 | tf_op jit(solution)/shard_map/ppermute | solution.py:15
  212.6 1.5 collective-permute-start.51
  215.4 4.2 %collective-permute-done.50 = bf16[160,1024]{1,0:T(8,128)(2,1)S(1)} collective-permute-done((bf16[160,1024]{1,0:T(8,128)(2,1)S(1)}, bf16[160,1024]{1,0:T(8,128)(2,1)S(1)}, u32[]{:S(2)}, u32[]{:S(2)}) %collective-permute-start.50) | collective-permute-done | bytes 327712 | tf_op jit(solution)/shard_map/ppermute | solution.py:15
  219.6 2.9 %collective-permute-done.49 = bf16[160,1024]{1,0:T(8,128)(2,1)S(1)} collective-permute-done((bf16[160,1024]{1,0:T(8,128)(2,1)S(1)}, bf16[160,1024]{1,0:T(8,128)(2,1)S(1)}, u32[]{:S(2)}, u32[]{:S(2)}) %collective-permute-start.49) | collective-permute-done | bytes 327712 | tf_op jit(solution)/shard_map/ppermute | solution.py:15
  222.6 8.5 %collective-permute-done.43 = bf16[320,1024]{1,0:T(8,128)(2,1)S(1)} collective-permute-done((bf16[320,1024]{1,0:T(8,128)(2,1)S(1)}, bf16[320,1024]{1,0:T(8,128)(2,1)S(1)}, u32[]{:S(2)}, u32[]{:S(2)}) %collective-permute-start.43) | collective-permute-done | bytes 655392 | tf_op jit(solution)/shard_map/ppermute | solution.py:15
  232.2 1.5 collective-permute-start.52
  238.3 3.5 %collective-permute-done.47 = bf16[160,1024]{1,0:T(8,128)(2,1)S(1)} collective-permute-done((bf16[160,1024]{1,0:T(8,128)(2,1)S(1)}, bf16[160,1024]{1,0:T(8,128)(2,1)S(1)}, u32[]{:S(2)}, u32[]{:S(2)}) %collective-permute-start.47) | collective-permute-done | bytes 327712 | tf_op jit(solution)/shard_map/ppermute | solution.py:15
  241.9 2.7 %collective-permute-done.48 = bf16[160,1024]{1,0:T(8,128)(2,1)S(1)} collective-permute-done((bf16[160,1024]{1,0:T(8,128)(2,1)S(1)}, bf16[160,1024]{1,0:T(8,128)(2,1)S(1)}, u32[]{:S(2)}, u32[]{:S(2)}) %collective-permute-start.48) | collective-permute-done | bytes 327712 | tf_op jit(solution)/shard_map/ppermute | solution.py:15
  244.6 2.9 %collective-permute-done.52 = bf16[320,1024]{1,0:T(8,128)(2,1)S(1)} collective-permute-done((bf16[320,1024]{1,0:T(8,128)(2,1)S(1)}, bf16[320,1024]{1,0:T(8,128)(2,1)S(1)}, u32[]{:S(2)}, u32[]{:S(2)}) %collective-permute-start.52) | collective-permute-done | bytes 655392 | tf_op jit(solution)/shard_map/ppermute | solution.py:20
  248.1 6.0 %collective-permute-done.45 = bf16[320,1024]{1,0:T(8,128)(2,1)S(1)} collective-permute-done((bf16[320,1024]{1,0:T(8,128)(2,1)S(1)}, bf16[320,1024]{1,0:T(8,128)(2,1)S(1)}, u32[]{:S(2)}, u32[]{:S(2)}) %collective-permute-start.45) | collective-permute-done | bytes 655392 | tf_op jit(solution)/shard_map/ppermute | solution.py:15
  254.1 2.3 collective-permute-start.46
  257.5 4.6 %collective-permute-done.53 = bf16[320,1024]{1,0:T(8,128)(2,1)S(1)} collective-permute-done((bf16[320,1024]{1,0:T(8,128)(2,1)S(1)}, bf16[320,1024]{1,0:T(8,128)(2,1)S(1)}, u32[]{:S(2)}, u32[]{:S(2)}) %collective-permute-start.53) | collective-permute-done | bytes 655392 | tf_op jit(solution)/shard_map/ppermute | solution.py:20
  262.1 1.5 collective-permute-done.55
  (174 shorter events, 55.6 us)
Async XLA Ops:
  5.7 5.5 %collective-permute-start.1 = (bf16[176,256]{1,0:T(8,128)(2,1)S(1)}, bf16[176,256]{1,0:T(8,128)(2,1)S(1)}, u32[]{:S(2)}, u32[]{:S(2)}) collective-permute-start(bf16[176,256]{1,0:T(8,128)(2,1)S(1)} %get-tuple-element.156), channel_id=1, source_target_pairs={{0,2},{1,3},{2,0},{3,1},{4,6},{5,7},{6,4},{7,5},{8,10},{9,11},{10,... | collective-permute-start | bytes 270344 | tf_op jit(solution)/shard_map/ppermute | solution.py:40
  5.8 19.3 %collective-permute-start.4 = (bf16[160,1024]{1,0:T(8,128)(2,1)S(1)}, bf16[160,1024]{1,0:T(8,128)(2,1)S(1)}, u32[]{:S(2)}, u32[]{:S(2)}) collective-permute-start(bf16[160,1024]{1,0:T(8,128)(2,1)S(1)} %get-tuple-element.128), channel_id=1, source_target_pairs={{0,2},{1,3},{2,0},{3,1},{4,6},{5,7},{6,4},{7,5},{8,10},{9,11},{10,... | collective-permute-start | bytes 983048 | tf_op jit(solution)/shard_map/ppermute | solution.py:40
  7.9 17.2 %collective-permute-start.5 = (bf16[160,1024]{1,0:T(8,128)(2,1)S(1)}, bf16[160,1024]{1,0:T(8,128)(2,1)S(1)}, u32[]{:S(2)}, u32[]{:S(2)}) collective-permute-start(bf16[160,1024]{1,0:T(8,128)(2,1)S(1)} %get-tuple-element.131), channel_id=1, source_target_pairs={{0,3},{1,2},{2,1},{3,0},{4,7},{5,6},{6,5},{7,4},{8,11},{9,10},{10,... | collective-permute-start | bytes 983048 | tf_op jit(solution)/shard_map/ppermute | solution.py:40
  19.4 5.7 %collective-permute-start.6 = (f32[16,160]{1,0:T(8,128)S(1)}, f32[16,160]{1,0:T(8,128)S(1)}, u32[]{:S(2)}, u32[]{:S(2)}) collective-permute-start(f32[16,160]{1,0:T(8,128)S(1)} %maximum_bitcast_fusion), channel_id=1, source_target_pairs={{0,8},{4,12},{8,16},{12,20},{16,24},{20,28},{24,0},{28,4},{1,9},{5... | collective-permute-start | bytes 30728 | tf_op jit(solution)/shard_map/ppermute | solution.py:259
  29.7 6.4 %collective-permute-start.3 = (bf16[160,1024]{1,0:T(8,128)(2,1)S(1)}, bf16[160,1024]{1,0:T(8,128)(2,1)S(1)}, u32[]{:S(2)}, u32[]{:S(2)}) collective-permute-start(bf16[160,1024]{1,0:T(8,128)(2,1)S(1)} %get-tuple-element.129), channel_id=1, source_target_pairs={{0,1},{1,0},{2,3},{3,2},{4,5},{5,4},{6,7},{7,6},{8,9},{9,8},{10,11... | collective-permute-start | bytes 983048 | tf_op jit(solution)/shard_map/ppermute | solution.py:40
  34.7 16.8 %collective-permute-start.10 = (bf16[160,2048]{1,0:T(8,128)(2,1)S(1)}, bf16[160,2048]{1,0:T(8,128)(2,1)S(1)}, u32[]{:S(2)}, u32[]{:S(2)}) collective-permute-start(bf16[160,2048]{1,0:T(8,128)(2,1)S(1)} %fusion), channel_id=1, source_target_pairs={{0,2},{1,3},{2,0},{3,1},{4,6},{5,7},{6,4},{7,5},{8,10},{9,11},{10,... | collective-permute-start | bytes 1966088 | tf_op jit(solution)/shard_map/ppermute | solution.py:15
  54.9 20.6 %collective-permute-start.16 = (bf16[320,1024]{1,0:T(8,128)(2,1)S(1)}, bf16[320,1024]{1,0:T(8,128)(2,1)S(1)}, u32[]{:S(2)}, u32[]{:S(2)}) collective-permute-start(bf16[320,1024]{1,0:T(8,128)(2,1)S(1)} %get-tuple-element.68.refs_0_), channel_id=1, source_target_pairs={{0,8},{4,12},{8,16},{12,20},{16,24},{20,28},{24,0},{28,4},{1,9},{5... | collective-permute-start | bytes 1966088 | tf_op jit(solution)/shard_map/ppermute | solution.py:20
  56.1 19.7 %collective-permute-start.14 = (bf16[320,1024]{1,0:T(8,128)(2,1)S(1)}, bf16[320,1024]{1,0:T(8,128)(2,1)S(1)}, u32[]{:S(2)}, u32[]{:S(2)}) collective-permute-start(bf16[320,1024]{1,0:T(8,128)(2,1)S(1)} %get-tuple-element.68.refs_0_), channel_id=1, source_target_pairs={{0,2},{1,3},{2,0},{3,1},{4,6},{5,7},{6,4},{7,5},{8,10},{9,11},{10,... | collective-permute-start | bytes 1966088 | tf_op jit(solution)/shard_map/ppermute | solution.py:15
  57.9 18.0 %collective-permute-start.13 = (bf16[320,1024]{1,0:T(8,128)(2,1)S(1)}, bf16[320,1024]{1,0:T(8,128)(2,1)S(1)}, u32[]{:S(2)}, u32[]{:S(2)}) collective-permute-start(bf16[320,1024]{1,0:T(8,128)(2,1)S(1)} %get-tuple-element.68.refs_0_), channel_id=1, source_target_pairs={{0,4},{4,0},{8,12},{12,8},{16,20},{20,16},{24,28},{28,24},{1,5},{5... | collective-permute-start | bytes 1966088 | tf_op jit(solution)/shard_map/ppermute | solution.py:15
  60.2 15.3 %collective-permute-start.12 = (f32[4,16,160]{2,1,0:T(8,128)S(1)}, f32[4,16,160]{2,1,0:T(8,128)S(1)}, u32[]{:S(2)}, u32[]{:S(2)}) collective-permute-start(f32[4,16,160]{2,1,0:T(8,128)S(1)} %pad_maximum_fusion.8), channel_id=1, source_target_pairs={{0,4},{4,0},{8,12},{12,8},{16,20},{20,16},{24,28},{28,24},{1,5},{5... | collective-permute-start | bytes 122888 | tf_op jit(solution)/shard_map/ppermute | solution.py:15
  75.5 18.2 %collective-permute-start.20 = (bf16[320,1024]{1,0:T(8,128)(2,1)S(1)}, bf16[320,1024]{1,0:T(8,128)(2,1)S(1)}, u32[]{:S(2)}, u32[]{:S(2)}) collective-permute-start(bf16[320,1024]{1,0:T(8,128)(2,1)S(1)} %collective-permute-done.16.refs_5_), channel_id=1, source_target_pairs={{0,2},{1,3},{2,0},{3,1},{4,6},{5,7},{6,4},{7,5},{8,10},{9,11},{10,... | collective-permute-start | bytes 1966088 | tf_op jit(solution)/shard_map/ppermute | solution.py:15
  75.9 17.9 %collective-permute-start.17 = (bf16[320,1024]{1,0:T(8,128)(2,1)S(1)}, bf16[320,1024]{1,0:T(8,128)(2,1)}, u32[]{:S(2)}, u32[]{:S(2)}) collective-permute-start(bf16[320,1024]{1,0:T(8,128)(2,1)S(1)} %collective-permute-done.16.refs_5_), channel_id=1, source_target_pairs={{0,8},{4,12},{8,16},{12,20},{16,24},{20,28},{24,0},{28,4},{1,9},{5... | collective-permute-start | bytes 1966088 | tf_op jit(solution)/shard_map/ppermute | solution.py:20
  77.5 16.3 %collective-permute-start.21 = (bf16[320,1024]{1,0:T(8,128)(2,1)S(1)}, bf16[320,1024]{1,0:T(8,128)(2,1)S(1)}, u32[]{:S(2)}, u32[]{:S(2)}) collective-permute-start(bf16[320,1024]{1,0:T(8,128)(2,1)S(1)} %collective-permute-done.16.refs_5_), channel_id=1, source_target_pairs={{0,4},{4,0},{8,12},{12,8},{16,20},{20,16},{24,28},{28,24},{1,5},{5... | collective-permute-start | bytes 1966088 | tf_op jit(solution)/shard_map/ppermute | solution.py:15
  79.0 14.7 %collective-permute-start.15 = (f32[4,2,16,160]{3,2,1,0:T(8,128)S(1)}, f32[4,2,16,160]{3,2,1,0:T(8,128)S(1)}, u32[]{:S(2)}, u32[]{:S(2)}) collective-permute-start(f32[4,2,16,160]{3,2,1,0:T(8,128)S(1)} %pad_maximum_fusion.7), channel_id=1, source_target_pairs={{0,2},{1,3},{2,0},{3,1},{4,6},{5,7},{6,4},{7,5},{8,10},{9,11},{10,... | collective-permute-start | bytes 245768 | tf_op jit(solution)/shard_map/ppermute | solution.py:15
  93.8 10.7 %collective-permute-start.18 = (bf16[160,1024]{1,0:T(8,128)(2,1)S(1)}, bf16[160,1024]{1,0:T(8,128)(2,1)S(1)}, u32[]{:S(2)}, u32[]{:S(2)}) collective-permute-start(bf16[160,1024]{1,0:T(8,128)(2,1)S(1)} %slice.152), channel_id=1, source_target_pairs={{0,2},{1,3},{2,0},{3,1},{4,6},{5,7},{6,4},{7,5},{8,10},{9,11},{10,... | collective-permute-start | bytes 983048 | tf_op jit(solution)/shard_map/ppermute | solution.py:15
  94.6 10.3 %collective-permute-start.19 = (bf16[160,1024]{1,0:T(8,128)(2,1)S(1)}, bf16[160,1024]{1,0:T(8,128)(2,1)S(1)}, u32[]{:S(2)}, u32[]{:S(2)}) collective-permute-start(bf16[160,1024]{1,0:T(8,128)(2,1)S(1)} %slice.153), channel_id=1, source_target_pairs={{0,4},{4,0},{8,12},{12,8},{16,20},{20,16},{24,28},{28,24},{1,5},{5... | collective-permute-start | bytes 983048 | tf_op jit(solution)/shard_map/ppermute | solution.py:15
  96.1 12.4 %collective-permute-start.22 = (bf16[160,1024]{1,0:T(8,128)(2,1)S(1)}, bf16[160,1024]{1,0:T(8,128)(2,1)S(1)}, u32[]{:S(2)}, u32[]{:S(2)}) collective-permute-start(bf16[160,1024]{1,0:T(8,128)(2,1)S(1)} %slice.159), channel_id=1, source_target_pairs={{0,2},{1,3},{2,0},{3,1},{4,6},{5,7},{6,4},{7,5},{8,10},{9,11},{10,... | collective-permute-start | bytes 983048 | tf_op jit(solution)/shard_map/ppermute | solution.py:15
  97.4 11.1 %collective-permute-start.23 = (bf16[160,1024]{1,0:T(8,128)(2,1)S(1)}, bf16[160,1024]{1,0:T(8,128)(2,1)S(1)}, u32[]{:S(2)}, u32[]{:S(2)}) collective-permute-start(bf16[160,1024]{1,0:T(8,128)(2,1)S(1)} %slice.160), channel_id=1, source_target_pairs={{0,4},{4,0},{8,12},{12,8},{16,20},{20,16},{24,28},{28,24},{1,5},{5... | collective-permute-start | bytes 983048 | tf_op jit(solution)/shard_map/ppermute | solution.py:15
  98.1 20.3 %collective-permute-start.26 = (bf16[320,1024]{1,0:T(8,128)(2,1)}, bf16[320,1024]{1,0:T(8,128)(2,1)S(1)}, u32[]{:S(2)}, u32[]{:S(2)}) collective-permute-start(bf16[320,1024]{1,0:T(8,128)(2,1)} %collective-permute-done.17.refs_0_), channel_id=1, source_target_pairs={{0,8},{4,12},{8,16},{12,20},{16,24},{20,28},{24,0},{28,4},{1,9},{5... | collective-permute-start | bytes 1966088 | tf_op jit(solution)/shard_map/ppermute | solution.py:20
  108.5 13.9 %collective-permute-start.25 = (bf16[320,1024]{1,0:T(8,128)(2,1)}, bf16[320,1024]{1,0:T(8,128)(2,1)S(1)}, u32[]{:S(2)}, u32[]{:S(2)}) collective-permute-start(bf16[320,1024]{1,0:T(8,128)(2,1)} %collective-permute-done.17.refs_0_), channel_id=1, source_target_pairs={{0,2},{1,3},{2,0},{3,1},{4,6},{5,7},{6,4},{7,5},{8,10},{9,11},{10,... | collective-permute-start | bytes 1966088 | tf_op jit(solution)/shard_map/ppermute | solution.py:15
  110.2 13.1 %collective-permute-start.24 = (bf16[320,1024]{1,0:T(8,128)(2,1)}, bf16[320,1024]{1,0:T(8,128)(2,1)S(1)}, u32[]{:S(2)}, u32[]{:S(2)}) collective-permute-start(bf16[320,1024]{1,0:T(8,128)(2,1)} %collective-permute-done.17.refs_0_), channel_id=1, source_target_pairs={{0,4},{4,0},{8,12},{12,8},{16,20},{20,16},{24,28},{28,24},{1,5},{5... | collective-permute-start | bytes 1966088 | tf_op jit(solution)/shard_map/ppermute | solution.py:15
  123.3 17.1 %collective-permute-start.29 = (bf16[320,1024]{1,0:T(8,128)(2,1)S(1)}, bf16[320,1024]{1,0:T(8,128)(2,1)S(1)}, u32[]{:S(2)}, u32[]{:S(2)}) collective-permute-start(bf16[320,1024]{1,0:T(8,128)(2,1)S(1)} %collective-permute-done.26.refs_5_), channel_id=1, source_target_pairs={{0,2},{1,3},{2,0},{3,1},{4,6},{5,7},{6,4},{7,5},{8,10},{9,11},{10,... | collective-permute-start | bytes 1966088 | tf_op jit(solution)/shard_map/ppermute | solution.py:15
  124.2 16.9 %collective-permute-start.28 = (bf16[320,1024]{1,0:T(8,128)(2,1)S(1)}, bf16[320,1024]{1,0:T(8,128)(2,1)S(1)}, u32[]{:S(2)}, u32[]{:S(2)}) collective-permute-start(bf16[320,1024]{1,0:T(8,128)(2,1)S(1)} %collective-permute-done.26.refs_5_), channel_id=1, source_target_pairs={{0,4},{4,0},{8,12},{12,8},{16,20},{20,16},{24,28},{28,24},{1,5},{5... | collective-permute-start | bytes 1966088 | tf_op jit(solution)/shard_map/ppermute | solution.py:15
  141.0 12.7 %collective-permute-start.32 = (bf16[512,2048]{1,0:T(8,128)(2,1)S(1)}, bf16[512,2048]{1,0:T(8,128)(2,1)S(1)}, u32[]{:S(2)}, u32[]{:S(2)}) collective-permute-start(bf16[512,2048]{1,0:T(8,128)(2,1)S(1)} %shard_map.128), channel_id=1, source_target_pairs={{0,1},{1,0},{2,3},{3,2},{4,5},{5,4},{6,7},{7,6},{8,9},{9,8},{10,11... | collective-permute-start | bytes 6291464 | tf_op jit(solution)/shard_map/ppermute | solution.py:15
  141.3 12.5 %collective-permute-start.31 = (bf16[160,1024]{1,0:T(8,128)(2,1)S(1)}, bf16[160,1024]{1,0:T(8,128)(2,1)S(1)}, u32[]{:S(2)}, u32[]{:S(2)}) collective-permute-start(bf16[160,1024]{1,0:T(8,128)(2,1)S(1)} %slice.162), channel_id=1, source_target_pairs={{0,4},{4,0},{8,12},{12,8},{16,20},{20,16},{24,28},{28,24},{1,5},{5... | collective-permute-start | bytes 983048 | tf_op jit(solution)/shard_map/ppermute | solution.py:15
  142.8 10.9 %collective-permute-start.30 = (bf16[160,1024]{1,0:T(8,128)(2,1)S(1)}, bf16[160,1024]{1,0:T(8,128)(2,1)S(1)}, u32[]{:S(2)}, u32[]{:S(2)}) collective-permute-start(bf16[160,1024]{1,0:T(8,128)(2,1)S(1)} %slice.161), channel_id=1, source_target_pairs={{0,2},{1,3},{2,0},{3,1},{4,6},{5,7},{6,4},{7,5},{8,10},{9,11},{10,... | collective-permute-start | bytes 983048 | tf_op jit(solution)/shard_map/ppermute | solution.py:15
  144.1 14.3 %collective-permute-start.34 = (bf16[160,1024]{1,0:T(8,128)(2,1)S(1)}, bf16[160,1024]{1,0:T(8,128)(2,1)S(1)}, u32[]{:S(2)}, u32[]{:S(2)}) collective-permute-start(bf16[160,1024]{1,0:T(8,128)(2,1)S(1)} %slice.169), channel_id=1, source_target_pairs={{0,4},{4,0},{8,12},{12,8},{16,20},{20,16},{24,28},{28,24},{1,5},{5... | collective-permute-start | bytes 983048 | tf_op jit(solution)/shard_map/ppermute | solution.py:15
  144.8 15.0 %collective-permute-start.33 = (bf16[160,1024]{1,0:T(8,128)(2,1)S(1)}, bf16[160,1024]{1,0:T(8,128)(2,1)S(1)}, u32[]{:S(2)}, u32[]{:S(2)}) collective-permute-start(bf16[160,1024]{1,0:T(8,128)(2,1)S(1)} %slice.168), channel_id=1, source_target_pairs={{0,2},{1,3},{2,0},{3,1},{4,6},{5,7},{6,4},{7,5},{8,10},{9,11},{10,... | collective-permute-start | bytes 983048 | tf_op jit(solution)/shard_map/ppermute | solution.py:15
  164.1 18.3 %collective-permute-start.35 = (bf16[320,1024]{1,0:T(8,128)(2,1)}, bf16[320,1024]{1,0:T(8,128)(2,1)S(1)}, u32[]{:S(2)}, u32[]{:S(2)}) collective-permute-start(bf16[320,1024]{1,0:T(8,128)(2,1)} %get-tuple-element.89), channel_id=1, source_target_pairs={{0,2},{1,3},{2,0},{3,1},{4,6},{5,7},{6,4},{7,5},{8,10},{9,11},{10,... | collective-permute-start | bytes 1966088 | tf_op jit(solution)/shard_map/ppermute | solution.py:15
  165.4 17.0 %collective-permute-start.37 = (bf16[320,1024]{1,0:T(8,128)(2,1)}, bf16[320,1024]{1,0:T(8,128)(2,1)S(1)}, u32[]{:S(2)}, u32[]{:S(2)}) collective-permute-start(bf16[320,1024]{1,0:T(8,128)(2,1)} %get-tuple-element.92), channel_id=1, source_target_pairs={{0,4},{4,0},{8,12},{12,8},{16,20},{20,16},{24,28},{28,24},{1,5},{5... | collective-permute-start | bytes 1966088 | tf_op jit(solution)/shard_map/ppermute | solution.py:15
  178.0 14.4 %collective-permute-start.40 = (bf16[512,2048]{1,0:T(8,128)(2,1)}, bf16[512,2048]{1,0:T(8,128)(2,1)S(1)}, u32[]{:S(2)}, u32[]{:S(2)}) collective-permute-start(bf16[512,2048]{1,0:T(8,128)(2,1)} %shard_map.132), channel_id=1, source_target_pairs={{0,1},{1,0},{2,3},{3,2},{4,5},{5,4},{6,7},{7,6},{8,9},{9,8},{10,11... | collective-permute-start | bytes 6291464 | tf_op jit(solution)/shard_map/ppermute | solution.py:15
  182.4 9.9 %collective-permute-start.38 = (bf16[160,1024]{1,0:T(8,128)(2,1)S(1)}, bf16[160,1024]{1,0:T(8,128)(2,1)S(1)}, u32[]{:S(2)}, u32[]{:S(2)}) collective-permute-start(bf16[160,1024]{1,0:T(8,128)(2,1)S(1)} %slice_add_fusion.15), channel_id=1, source_target_pairs={{0,4},{4,0},{8,12},{12,8},{16,20},{20,16},{24,28},{28,24},{1,5},{5... | collective-permute-start | bytes 983048 | tf_op jit(solution)/shard_map/ppermute | solution.py:15
  183.1 9.3 %collective-permute-start.39 = (bf16[160,1024]{1,0:T(8,128)(2,1)S(1)}, bf16[160,1024]{1,0:T(8,128)(2,1)S(1)}, u32[]{:S(2)}, u32[]{:S(2)}) collective-permute-start(bf16[160,1024]{1,0:T(8,128)(2,1)S(1)} %slice_add_fusion.14), channel_id=1, source_target_pairs={{0,2},{1,3},{2,0},{3,1},{4,6},{5,7},{6,4},{7,5},{8,10},{9,11},{10,... | collective-permute-start | bytes 983048 | tf_op jit(solution)/shard_map/ppermute | solution.py:15
  193.3 15.5 %collective-permute-start.42 = (bf16[320,1024]{1,0:T(8,128)(2,1)S(1)}, bf16[320,1024]{1,0:T(8,128)(2,1)S(1)}, u32[]{:S(2)}, u32[]{:S(2)}) collective-permute-start(bf16[320,1024]{1,0:T(8,128)(2,1)S(1)} %get-tuple-element.107), channel_id=1, source_target_pairs={{0,4},{4,0},{8,12},{12,8},{16,20},{20,16},{24,28},{28,24},{1,5},{5... | collective-permute-start | bytes 1966088 | tf_op jit(solution)/shard_map/ppermute | solution.py:15
  194.9 15.7 %collective-permute-start.41 = (bf16[320,1024]{1,0:T(8,128)(2,1)S(1)}, bf16[320,1024]{1,0:T(8,128)(2,1)S(1)}, u32[]{:S(2)}, u32[]{:S(2)}) collective-permute-start(bf16[320,1024]{1,0:T(8,128)(2,1)S(1)} %get-tuple-element.105), channel_id=1, source_target_pairs={{0,2},{1,3},{2,0},{3,1},{4,6},{5,7},{6,4},{7,5},{8,10},{9,11},{10,... | collective-permute-start | bytes 1966088 | tf_op jit(solution)/shard_map/ppermute | solution.py:15
  208.8 10.7 %collective-permute-start.50 = (bf16[160,1024]{1,0:T(8,128)(2,1)S(1)}, bf16[160,1024]{1,0:T(8,128)(2,1)S(1)}, u32[]{:S(2)}, u32[]{:S(2)}) collective-permute-start(bf16[160,1024]{1,0:T(8,128)(2,1)S(1)} %slice_add_fusion.4), channel_id=1, source_target_pairs={{0,2},{1,3},{2,0},{3,1},{4,6},{5,7},{6,4},{7,5},{8,10},{9,11},{10,... | collective-permute-start | bytes 983048 | tf_op jit(solution)/shard_map/ppermute | solution.py:15
  210.6 20.5 %collective-permute-start.43 = (bf16[320,1024]{1,0:T(8,128)(2,1)S(1)}, bf16[320,1024]{1,0:T(8,128)(2,1)S(1)}, u32[]{:S(2)}, u32[]{:S(2)}) collective-permute-start(bf16[320,1024]{1,0:T(8,128)(2,1)S(1)} %get-tuple-element.108), channel_id=1, source_target_pairs={{0,2},{1,3},{2,0},{3,1},{4,6},{5,7},{6,4},{7,5},{8,10},{9,11},{10,... | collective-permute-start | bytes 1966088 | tf_op jit(solution)/shard_map/ppermute | solution.py:15
  211.8 10.7 %collective-permute-start.49 = (bf16[160,1024]{1,0:T(8,128)(2,1)S(1)}, bf16[160,1024]{1,0:T(8,128)(2,1)S(1)}, u32[]{:S(2)}, u32[]{:S(2)}) collective-permute-start(bf16[160,1024]{1,0:T(8,128)(2,1)S(1)} %slice_add_fusion.6), channel_id=1, source_target_pairs={{0,4},{4,0},{8,12},{12,8},{16,20},{20,16},{24,28},{28,24},{1,5},{5... | collective-permute-start | bytes 983048 | tf_op jit(solution)/shard_map/ppermute | solution.py:15
  212.6 19.4 %collective-permute-start.51 = (bf16[320,1024]{1,0:T(8,128)(2,1)S(1)}, bf16[320,1024]{1,0:T(8,128)(2,1)S(1)}, u32[]{:S(2)}, u32[]{:S(2)}) collective-permute-start(bf16[320,1024]{1,0:T(8,128)(2,1)S(1)} %pad_maximum_fusion), channel_id=1, source_target_pairs={{0,8},{4,12},{8,16},{12,20},{16,24},{20,28},{24,0},{28,4},{1,9},{5... | collective-permute-start | bytes 1966088 | tf_op jit(solution)/shard_map/ppermute | solution.py:20
  214.1 19.7 %collective-permute-start.44 = (bf16[320,1024]{1,0:T(8,128)(2,1)S(1)}, bf16[320,1024]{1,0:T(8,128)(2,1)S(1)}, u32[]{:S(2)}, u32[]{:S(2)}) collective-permute-start(bf16[320,1024]{1,0:T(8,128)(2,1)S(1)} %get-tuple-element.110), channel_id=1, source_target_pairs={{0,4},{4,0},{8,12},{12,8},{16,20},{20,16},{24,28},{28,24},{1,5},{5... | collective-permute-start | bytes 1966088 | tf_op jit(solution)/shard_map/ppermute | solution.py:15
  231.1 10.7 %collective-permute-start.47 = (bf16[160,1024]{1,0:T(8,128)(2,1)S(1)}, bf16[160,1024]{1,0:T(8,128)(2,1)S(1)}, u32[]{:S(2)}, u32[]{:S(2)}) collective-permute-start(bf16[160,1024]{1,0:T(8,128)(2,1)S(1)} %slice_add_fusion.10), channel_id=1, source_target_pairs={{0,4},{4,0},{8,12},{12,8},{16,20},{20,16},{24,28},{28,24},{1,5},{5... | collective-permute-start | bytes 983048 | tf_op jit(solution)/shard_map/ppermute | solution.py:15
  232.2 15.3 %collective-permute-start.52 = (bf16[320,1024]{1,0:T(8,128)(2,1)S(1)}, bf16[320,1024]{1,0:T(8,128)(2,1)S(1)}, u32[]{:S(2)}, u32[]{:S(2)}) collective-permute-start(bf16[320,1024]{1,0:T(8,128)(2,1)S(1)} %maximum_add_fusion.1), channel_id=1, source_target_pairs={{0,8},{4,12},{8,16},{12,20},{16,24},{20,28},{24,0},{28,4},{1,9},{5... | collective-permute-start | bytes 1966088 | tf_op jit(solution)/shard_map/ppermute | solution.py:20
  233.8 10.7 %collective-permute-start.48 = (bf16[160,1024]{1,0:T(8,128)(2,1)S(1)}, bf16[160,1024]{1,0:T(8,128)(2,1)S(1)}, u32[]{:S(2)}, u32[]{:S(2)}) collective-permute-start(bf16[160,1024]{1,0:T(8,128)(2,1)S(1)} %slice_add_fusion.8), channel_id=1, source_target_pairs={{0,2},{1,3},{2,0},{3,1},{4,6},{5,7},{6,4},{7,5},{8,10},{9,11},{10,... | collective-permute-start | bytes 983048 | tf_op jit(solution)/shard_map/ppermute | solution.py:15
  235.9 18.2 %collective-permute-start.45 = (bf16[320,1024]{1,0:T(8,128)(2,1)S(1)}, bf16[320,1024]{1,0:T(8,128)(2,1)S(1)}, u32[]{:S(2)}, u32[]{:S(2)}) collective-permute-start(bf16[320,1024]{1,0:T(8,128)(2,1)S(1)} %get-tuple-element.111), channel_id=1, source_target_pairs={{0,2},{1,3},{2,0},{3,1},{4,6},{5,7},{6,4},{7,5},{8,10},{9,11},{10,... | collective-permute-start | bytes 1966088 | tf_op jit(solution)/shard_map/ppermute | solution.py:15
  236.9 19.6 %collective-permute-start.54 = (bf16[320,1024]{1,0:T(8,128)(2,1)S(1)}, bf16[320,1024]{1,0:T(8,128)(2,1)S(1)}, u32[]{:S(2)}, u32[]{:S(2)}) collective-permute-start(bf16[320,1024]{1,0:T(8,128)(2,1)S(1)} %get-tuple-element.122), channel_id=1, source_target_pairs={{0,4},{4,0},{8,12},{12,8},{16,20},{20,16},{24,28},{28,24},{1,5},{5... | collective-permute-start | bytes 1966088 | tf_op jit(solution)/shard_map/ppermute | solution.py:15
  247.8 14.4 %collective-permute-start.53 = (bf16[320,1024]{1,0:T(8,128)(2,1)S(1)}, bf16[320,1024]{1,0:T(8,128)(2,1)S(1)}, u32[]{:S(2)}, u32[]{:S(2)}) collective-permute-start(bf16[320,1024]{1,0:T(8,128)(2,1)S(1)} %maximum_add_fusion), channel_id=1, source_target_pairs={{0,8},{4,12},{8,16},{12,20},{16,24},{20,28},{24,0},{28,4},{1,9},{5... | collective-permute-start | bytes 1966088 | tf_op jit(solution)/shard_map/ppermute | solution.py:20
  254.1 8.0 %collective-permute-start.46 = (bf16[160,1024]{1,0:T(8,128)(2,1)S(1)}, bf16[160,1024]{1,0:T(8,128)(2,1)S(1)}, u32[]{:S(2)}, u32[]{:S(2)}) collective-permute-start(bf16[160,1024]{1,0:T(8,128)(2,1)S(1)} %slice_add_fusion.12), channel_id=1, source_target_pairs={{0,4},{4,0},{8,12},{12,8},{16,20},{20,16},{24,28},{28,24},{1,5},{5... | collective-permute-start | bytes 983048 | tf_op jit(solution)/shard_map/ppermute | solution.py:15
  256.5 7.1 %collective-permute-start.55 = (bf16[160,1024]{1,0:T(8,128)(2,1)S(1)}, bf16[160,1024]{1,0:T(8,128)(2,1)S(1)}, u32[]{:S(2)}, u32[]{:S(2)}) collective-permute-start(bf16[160,1024]{1,0:T(8,128)(2,1)S(1)} %slice_add_fusion.1), channel_id=1, source_target_pairs={{0,2},{1,3},{2,0},{3,1},{4,6},{5,7},{6,4},{7,5},{8,10},{9,11},{10,... | collective-permute-start | bytes 983048 | tf_op jit(solution)/shard_map/ppermute | solution.py:15
  (30 other events, 264.9 us)
